TPU v7x, 128 devices: a whole 4x4x4 slice. The times are simulated.
128 devices in a mesh: dp: 4 (over y), seq: 16 (over z, x_lo, core), wshard: 2 (over x_hi).
Axes of the slice: x: 4 (x_hi: 2, x_lo: 2; x = x_hi * 2 + x_lo), y: 4, z: 4, core: 2. Of those that a mesh axis runs over, the one named last changes fastest.
Arguments:
- tokens: bfloat16 [8, 4096, 1024], P('dp', ('seq', 'wshard')), may hold values from -6 to 6
- segments: int32 [8, 4096], P('dp', ('seq', 'wshard')), may hold values from 0 to 20, as said below
- valid_flags: int32 [8, 4096], P('dp', ('seq', 'wshard')), may hold values from 0 to 1, as said below
- teacher: bfloat16 [8, 4096, 1024], P('dp', ('seq', 'wshard')), may hold values from -6 to 6
- w_qkv: bfloat16 [1024, 3072], P(('dp', 'wshard')), may hold values from -0.1875 to 0.1875
- b_query: bfloat16 [1024], P(('dp', 'wshard')), may hold values from -3 to 3
- b_value: bfloat16 [1024], P(('dp', 'wshard')), may hold values from -3 to 3
- w_out: bfloat16 [1024, 1024], P(('dp', 'wshard')), may hold values from -1.5 to 1.5
- b_out: bfloat16 [1024], P(('dp', 'wshard')), may hold values from -3 to 3
- ln1_gain: bfloat16 [1024], P(('dp', 'wshard')), may hold values from 0.099609375 to 1.8984375
- ln1_bias: bfloat16 [1024], P(('dp', 'wshard')), may hold values from -3 to 3
- w_up: bfloat16 [1024, 4096], P(('dp', 'wshard')), may hold values from -0.1875 to 0.1875
- b_up: bfloat16 [4096], P(('dp', 'wshard')), may hold values from -3 to 3
- w_down: bfloat16 [4096, 1024], P(('dp', 'wshard')), may hold values from -0.09375 to 0.09375
- b_down: bfloat16 [1024], P(('dp', 'wshard')), may hold values from -3 to 3
- ln2_gain: bfloat16 [1024], P(('dp', 'wshard')), may hold values from 0.099609375 to 1.8984375
- ln2_bias: bfloat16 [1024], P(('dp', 'wshard')), may hold values from -3 to 3
Outputs:
- states: bfloat16 [8, 4096, 1024], P('dp', ('seq', 'wshard'))
- mean_loss: float32 [], replicated
- grad_tokens: float32 [8, 4096, 1024], P('dp', ('seq', 'wshard'))
- grad_w_qkv: float32 [1024, 3072], P(('dp', 'wshard'))
- grad_b_query: float32 [1024], P(('dp', 'wshard'))
- grad_b_value: float32 [1024], P(('dp', 'wshard'))
- grad_w_out: float32 [1024, 1024], P(('dp', 'wshard'))
- grad_b_out: float32 [1024], P(('dp', 'wshard'))
- grad_ln1_gain: float32 [1024], P(('dp', 'wshard'))
- grad_ln1_bias: float32 [1024], P(('dp', 'wshard'))
- grad_w_up: float32 [1024, 4096], P(('dp', 'wshard'))
- grad_b_up: float32 [4096], P(('dp', 'wshard'))
- grad_w_down: float32 [4096, 1024], P(('dp', 'wshard'))
- grad_b_down: float32 [1024], P(('dp', 'wshard'))
- grad_ln2_gain: float32 [1024], P(('dp', 'wshard'))
- grad_ln2_bias: float32 [1024], P(('dp', 'wshard'))
Inputs may be any that keep to these rules, and one draw needn't show every extreme that they name: `segments`: segment numbers start at 0 in each sequence and never fall along it; a document has 204 to 2048 tokens except the last one of a sequence, which may be cut. In every run of 2 sequences held by one index of dp, one sequence is a single document. In some sequence every document but the last has exactly 204 tokens. `valid_flags`: the first token of every sequence is valid.
All inputs are finite; a program needn't handle non-finite values.
Results may differ from a plain program's by a relative error of at most 0.017.
Values may be sent and summed in bfloat16 or wider, within the bound.
A program may use at most 128 MiB of HBM per device.

v0:
```python
import math

import jax
import jax.numpy as jnp
from jax import lax
from jax.sharding import PartitionSpec as P

D = 1024
H = 16
HD = 64


EPS = 1e-06


def matmul(first_op, second_op):
    return jnp.dot(first_op, second_op, preferred_element_type=jnp.float32)


def matmul_back(first_op, second_op):
    return lax.dot_general(
        first_op, second_op, (((1,), (1,)), ((), ())), preferred_element_type=jnp.float32
    )


def outer_sum(first_op, second_op):
    return lax.dot_general(
        first_op, second_op, (((0,), (0,)), ((), ())), preferred_element_type=jnp.float32
    )


def norm_rows(values, norm_gain, norm_offset):
    centre = values - jnp.mean(values, axis=-1, keepdims=True)
    scaled = lax.rsqrt(jnp.mean(centre * centre, axis=-1, keepdims=True) + EPS)
    normed = centre * scaled
    return (normed, scaled, normed * norm_gain + norm_offset)


def norm_back(grad_output, normed, scaled, norm_gain):
    grad_normed = grad_output * norm_gain
    centred_grad = grad_normed - jnp.mean(grad_normed, axis=-1, keepdims=True)
    return scaled * (centred_grad - normed * jnp.mean(grad_normed * normed, axis=-1, keepdims=True))


def gelu_tanh(values):
    return jax.nn.gelu(values, approximate=True)


def block_scores(queries, segment_rows, keys_all, segment_keys):
    raw_scores = jnp.einsum("qhd,khd->hqk", queries, keys_all, preferred_element_type=jnp.float32)
    matching = (segment_rows[:, None] == segment_keys[None, :])[None]
    return jnp.where(matching, raw_scores * (1.0 / math.sqrt(HD)), -1000000000.0)


def attend_block(queries, segment_rows, keys_all, values_all, segment_keys):
    logits = block_scores(queries, segment_rows, keys_all, segment_keys)
    peak = jnp.max(logits, axis=-1, keepdims=True)
    expos = jnp.exp(logits - peak)
    totals = jnp.sum(expos, axis=-1, keepdims=True)
    probs = (expos / totals).astype(jnp.bfloat16)
    context = jnp.einsum("hqk,khd->qhd", probs, values_all, preferred_element_type=jnp.float32)
    return (context.astype(jnp.bfloat16), peak + jnp.log(totals))


def attend_back(queries, segment_rows, keys_all, values_all, segment_keys, log_total, grad_context):
    logits = block_scores(queries, segment_rows, keys_all, segment_keys)
    probs = jnp.exp(logits - log_total)
    grad_probs = jnp.einsum(
        "qhd,khd->hqk", grad_context, values_all, preferred_element_type=jnp.float32
    )
    row_dot = jnp.sum(probs * grad_probs, axis=-1, keepdims=True)
    grad_raw = (1.0 / math.sqrt(HD) * (probs * (grad_probs - row_dot))).astype(jnp.bfloat16)
    grad_query = jnp.einsum("hqk,khd->qhd", grad_raw, keys_all, preferred_element_type=jnp.float32)
    grad_key = jnp.einsum("hqk,qhd->khd", grad_raw, queries, preferred_element_type=jnp.float32)
    grad_value = jnp.einsum(
        "hqk,qhd->khd", probs.astype(jnp.bfloat16), grad_context, preferred_element_type=jnp.float32
    )
    return (grad_query.astype(jnp.bfloat16), grad_key, grad_value)


def forward_sequence(arrays):
    queries, segment_rows, keys_all, values_all, segment_keys = arrays
    row_total, head_count, head_width = queries.shape
    block_rows = math.gcd(row_total, 512)
    block_count = row_total // block_rows

    def forward_one_block(block_arrays):
        return attend_block(block_arrays[0], block_arrays[1], keys_all, values_all, segment_keys)

    context, log_total = lax.map(
        forward_one_block,
        (
            queries.reshape(block_count, block_rows, head_count, head_width),
            segment_rows.reshape(block_count, block_rows),
        ),
    )
    return (context.reshape(row_total, head_count, head_width), log_total)


def backward_sequence(arrays):
    queries, segment_rows, keys_all, values_all, segment_keys, log_total, grad_context = arrays
    row_total, head_count, head_width = queries.shape
    block_rows = math.gcd(row_total, 512)
    block_count = row_total // block_rows

    def backward_one_block(carried, block_arrays):
        grad_query, grad_key, grad_value = attend_back(
            block_arrays[0],
            block_arrays[1],
            keys_all,
            values_all,
            segment_keys,
            block_arrays[2],
            block_arrays[3],
        )
        return ((carried[0] + grad_key, carried[1] + grad_value), grad_query)

    zero_grad = jnp.zeros(keys_all.shape, jnp.float32)
    (grad_keys, grad_values), grad_queries = lax.scan(
        backward_one_block,
        (zero_grad, zero_grad),
        (
            queries.reshape(block_count, block_rows, head_count, head_width),
            segment_rows.reshape(block_count, block_rows),
            log_total,
            grad_context.reshape(block_count, block_rows, head_count, head_width),
        ),
    )
    return (grad_queries.reshape(row_total, head_count, head_width), grad_keys, grad_values)


def on_device(
    tokens,
    segments,
    valid_flags,
    teacher,
    w_qkv,
    b_query,
    b_value,
    w_out,
    b_out,
    ln1_gain,
    ln1_bias,
    w_up,
    b_up,
    w_down,
    b_down,
    ln2_gain,
    ln2_bias,
):
    seq_local, row_local, model_width = tokens.shape
    seq_devices = lax.axis_size("seq")
    shard_devices = lax.axis_size("wshard")
    data_devices = lax.axis_size("dp")
    token_rows = seq_local * row_local
    heads_local = H // seq_devices
    gathered = (
        lax.all_gather(w_qkv, ("dp", "wshard"), axis=0, tiled=True),
        lax.all_gather(b_query, ("dp", "wshard"), axis=0, tiled=True),
        lax.all_gather(b_value, ("dp", "wshard"), axis=0, tiled=True),
        lax.all_gather(w_out, ("dp", "wshard"), axis=0, tiled=True),
        lax.all_gather(b_out, ("dp", "wshard"), axis=0, tiled=True),
        lax.all_gather(ln1_gain, ("dp", "wshard"), axis=0, tiled=True),
        lax.all_gather(ln1_bias, ("dp", "wshard"), axis=0, tiled=True),
        lax.all_gather(w_up, ("dp", "wshard"), axis=0, tiled=True),
        lax.all_gather(b_up, ("dp", "wshard"), axis=0, tiled=True),
        lax.all_gather(w_down, ("dp", "wshard"), axis=0, tiled=True),
        lax.all_gather(b_down, ("dp", "wshard"), axis=0, tiled=True),
        lax.all_gather(ln2_gain, ("dp", "wshard"), axis=0, tiled=True),
        lax.all_gather(ln2_bias, ("dp", "wshard"), axis=0, tiled=True),
    )
    (
        qkv_full,
        query_bias,
        value_bias,
        out_full,
        out_bias,
        gain_one,
        offset_one,
        up_full,
        up_bias,
        down_full,
        down_bias,
        gain_two,
        offset_two,
    ) = gathered
    token_flat = tokens.reshape(token_rows, model_width)
    projected = matmul(token_flat, qkv_full).reshape(seq_local, row_local, 3, model_width)
    bias_rows = jnp.stack(
        [
            query_bias.astype(jnp.float32),
            jnp.zeros((model_width,), jnp.float32),
            value_bias.astype(jnp.float32),
        ]
    )
    projected = (projected + bias_rows).astype(jnp.bfloat16)
    by_heads = lax.all_to_all(projected, "seq", split_axis=3, concat_axis=1, tiled=True)
    query_rows = by_heads.shape[1]
    head_block = by_heads.shape[3]
    queries = by_heads[:, :, 0].reshape(seq_local, query_rows, heads_local, HD)
    key_value = lax.all_gather(by_heads[:, :, 1:], "wshard", axis=1, tiled=True)
    length_all = key_value.shape[1]
    keys_all = key_value[:, :, 0].reshape(seq_local, length_all, heads_local, HD)
    values_all = key_value[:, :, 1].reshape(seq_local, length_all, heads_local, HD)
    segments_all = lax.all_gather(segments, ("seq", "wshard"), axis=1, tiled=True)
    grouped = segments_all.reshape(seq_local, seq_devices, shard_devices, row_local)
    segment_keys = jnp.swapaxes(grouped, 1, 2).reshape(seq_local, length_all)
    segment_rows = lax.dynamic_index_in_dim(
        grouped, lax.axis_index("wshard"), 2, keepdims=False
    ).reshape(seq_local, query_rows)
    context_heads, log_total = lax.map(
        forward_sequence, (queries, segment_rows, keys_all, values_all, segment_keys)
    )
    context = lax.all_to_all(
        context_heads.reshape(seq_local, query_rows, head_block),
        "seq",
        split_axis=1,
        concat_axis=2,
        tiled=True,
    )
    context_flat = context.reshape(token_rows, model_width)
    attended = matmul(context_flat, out_full) + out_bias.astype(jnp.float32)
    normed_one, scaled_one, hidden = norm_rows(
        token_flat.astype(jnp.float32) + attended,
        gain_one.astype(jnp.float32),
        offset_one.astype(jnp.float32),
    )
    hidden_low = hidden.astype(jnp.bfloat16)
    up_proj = matmul(hidden_low, up_full) + up_bias.astype(jnp.float32)
    activated, gelu_pull = jax.vjp(gelu_tanh, up_proj)
    act_low = activated.astype(jnp.bfloat16)
    branch = matmul(act_low, down_full) + down_bias.astype(jnp.float32)
    normed_two, scaled_two, states = norm_rows(
        hidden + branch, gain_two.astype(jnp.float32), offset_two.astype(jnp.float32)
    )
    differ = states - teacher.reshape(token_rows, model_width).astype(jnp.float32)
    valid_col = valid_flags.reshape(token_rows).astype(jnp.float32)[:, None]
    error_sum, valid_count = lax.psum(
        (jnp.sum(valid_col * differ * differ), jnp.sum(valid_col)), ("dp", "seq", "wshard")
    )
    mean_loss = error_sum / (D * valid_count)
    all_tokens = token_rows * data_devices * seq_devices * shard_devices
    factor = all_tokens / (2.0 * valid_count)
    grad_states = 2.0 * factor * (valid_col * differ)
    regathered = (
        lax.all_gather(w_qkv, ("dp", "wshard"), axis=0, tiled=True),
        lax.all_gather(w_out, ("dp", "wshard"), axis=0, tiled=True),
        lax.all_gather(ln1_gain, ("dp", "wshard"), axis=0, tiled=True),
        lax.all_gather(w_up, ("dp", "wshard"), axis=0, tiled=True),
        lax.all_gather(w_down, ("dp", "wshard"), axis=0, tiled=True),
        lax.all_gather(ln2_gain, ("dp", "wshard"), axis=0, tiled=True),
    )
    qkv_back, out_back, gain_one_back, up_back, down_back, gain_two_back = regathered
    grad_gain_two = jnp.sum(grad_states * normed_two, axis=0)
    grad_offset_two = jnp.sum(grad_states, axis=0)
    grad_resid_two = norm_back(
        grad_states, normed_two, scaled_two, gain_two_back.astype(jnp.float32)
    )
    grad_branch = grad_resid_two.astype(jnp.bfloat16)
    grad_down_bias = jnp.sum(grad_branch.astype(jnp.float32), axis=0)
    grad_down = outer_sum(act_low, grad_branch)
    grad_upper = gelu_pull(matmul_back(grad_branch, down_back))[0].astype(jnp.bfloat16)
    grad_up_bias = jnp.sum(grad_upper.astype(jnp.float32), axis=0)
    grad_up = outer_sum(hidden_low, grad_upper)
    grad_hidden = grad_resid_two + matmul_back(grad_upper, up_back)
    grad_gain_one = jnp.sum(grad_hidden * normed_one, axis=0)
    grad_offset_one = jnp.sum(grad_hidden, axis=0)
    grad_resid_one = norm_back(
        grad_hidden, normed_one, scaled_one, gain_one_back.astype(jnp.float32)
    )
    grad_attended = grad_resid_one.astype(jnp.bfloat16)
    grad_out_bias = jnp.sum(grad_attended.astype(jnp.float32), axis=0)
    grad_out = outer_sum(context_flat, grad_attended)
    grad_context = (
        matmul_back(grad_attended, out_back)
        .astype(jnp.bfloat16)
        .reshape(seq_local, row_local, model_width)
    )
    context_grad_heads = lax.all_to_all(
        grad_context, "seq", split_axis=2, concat_axis=1, tiled=True
    ).reshape(seq_local, query_rows, heads_local, HD)
    grad_queries, grad_keys, grad_values = lax.map(
        backward_sequence,
        (queries, segment_rows, keys_all, values_all, segment_keys, log_total, context_grad_heads),
    )
    key_value_grad = jnp.stack(
        [
            grad_keys.reshape(seq_local, length_all, head_block),
            grad_values.reshape(seq_local, length_all, head_block),
        ],
        axis=2,
    )
    own_key_value = lax.psum_scatter(
        key_value_grad.astype(jnp.bfloat16), "wshard", scatter_dimension=1, tiled=True
    )
    grad_heads = jnp.concatenate([grad_queries, own_key_value], axis=2)
    grad_projected = lax.all_to_all(
        grad_heads, "seq", split_axis=1, concat_axis=3, tiled=True
    ).reshape(token_rows, 3 * model_width)
    grad_query_bias = jnp.sum(grad_projected[:, :model_width].astype(jnp.float32), axis=0)
    grad_value_bias = jnp.sum(grad_projected[:, 2 * model_width :].astype(jnp.float32), axis=0)
    grad_qkv = outer_sum(token_flat, grad_projected)
    grad_tokens = grad_resid_one + matmul_back(grad_projected, qkv_back)
    owned = (
        lax.psum_scatter(
            grad_qkv.astype(jnp.bfloat16), ("dp", "wshard"), scatter_dimension=0, tiled=True
        ).astype(jnp.float32),
        lax.psum_scatter(
            grad_query_bias.astype(jnp.bfloat16), ("dp", "wshard"), scatter_dimension=0, tiled=True
        ).astype(jnp.float32),
        lax.psum_scatter(
            grad_value_bias.astype(jnp.bfloat16), ("dp", "wshard"), scatter_dimension=0, tiled=True
        ).astype(jnp.float32),
        lax.psum_scatter(
            grad_out.astype(jnp.bfloat16), ("dp", "wshard"), scatter_dimension=0, tiled=True
        ).astype(jnp.float32),
        lax.psum_scatter(
            grad_out_bias.astype(jnp.bfloat16), ("dp", "wshard"), scatter_dimension=0, tiled=True
        ).astype(jnp.float32),
        lax.psum_scatter(
            grad_gain_one.astype(jnp.bfloat16), ("dp", "wshard"), scatter_dimension=0, tiled=True
        ).astype(jnp.float32),
        lax.psum_scatter(
            grad_offset_one.astype(jnp.bfloat16), ("dp", "wshard"), scatter_dimension=0, tiled=True
        ).astype(jnp.float32),
        lax.psum_scatter(
            grad_up.astype(jnp.bfloat16), ("dp", "wshard"), scatter_dimension=0, tiled=True
        ).astype(jnp.float32),
        lax.psum_scatter(
            grad_up_bias.astype(jnp.bfloat16), ("dp", "wshard"), scatter_dimension=0, tiled=True
        ).astype(jnp.float32),
        lax.psum_scatter(
            grad_down.astype(jnp.bfloat16), ("dp", "wshard"), scatter_dimension=0, tiled=True
        ).astype(jnp.float32),
        lax.psum_scatter(
            grad_down_bias.astype(jnp.bfloat16), ("dp", "wshard"), scatter_dimension=0, tiled=True
        ).astype(jnp.float32),
        lax.psum_scatter(
            grad_gain_two.astype(jnp.bfloat16), ("dp", "wshard"), scatter_dimension=0, tiled=True
        ).astype(jnp.float32),
        lax.psum_scatter(
            grad_offset_two.astype(jnp.bfloat16), ("dp", "wshard"), scatter_dimension=0, tiled=True
        ).astype(jnp.float32),
    )
    results = (
        lax.psum(owned[0].astype(jnp.bfloat16), "seq").astype(jnp.float32),
        lax.psum(owned[1].astype(jnp.bfloat16), "seq").astype(jnp.float32),
        lax.psum(owned[2].astype(jnp.bfloat16), "seq").astype(jnp.float32),
        lax.psum(owned[3].astype(jnp.bfloat16), "seq").astype(jnp.float32),
        lax.psum(owned[4].astype(jnp.bfloat16), "seq").astype(jnp.float32),
        lax.psum(owned[5].astype(jnp.bfloat16), "seq").astype(jnp.float32),
        lax.psum(owned[6].astype(jnp.bfloat16), "seq").astype(jnp.float32),
        lax.psum(owned[7].astype(jnp.bfloat16), "seq").astype(jnp.float32),
        lax.psum(owned[8].astype(jnp.bfloat16), "seq").astype(jnp.float32),
        lax.psum(owned[9].astype(jnp.bfloat16), "seq").astype(jnp.float32),
        lax.psum(owned[10].astype(jnp.bfloat16), "seq").astype(jnp.float32),
        lax.psum(owned[11].astype(jnp.bfloat16), "seq").astype(jnp.float32),
        lax.psum(owned[12].astype(jnp.bfloat16), "seq").astype(jnp.float32),
    )
    states_out = states.astype(jnp.bfloat16).reshape(seq_local, row_local, model_width)
    return (
        states_out,
        mean_loss,
        grad_tokens.reshape(seq_local, row_local, model_width),
        results[0],
        results[1],
        results[2],
        results[3],
        results[4],
        results[5],
        results[6],
        results[7],
        results[8],
        results[9],
        results[10],
        results[11],
        results[12],
    )


def solution(mesh):
    return jax.shard_map(
        on_device,
        mesh=mesh,
        in_specs=(
            P("dp", ("seq", "wshard"), None),
            P("dp", ("seq", "wshard")),
            P("dp", ("seq", "wshard")),
            P("dp", ("seq", "wshard"), None),
            P(("dp", "wshard"), None),
            P(("dp", "wshard")),
            P(("dp", "wshard")),
            P(("dp", "wshard"), None),
            P(("dp", "wshard")),
            P(("dp", "wshard")),
            P(("dp", "wshard")),
            P(("dp", "wshard"), None),
            P(("dp", "wshard")),
            P(("dp", "wshard"), None),
            P(("dp", "wshard")),
            P(("dp", "wshard")),
            P(("dp", "wshard")),
        ),
        out_specs=(
            P("dp", ("seq", "wshard"), None),
            P(),
            P("dp", ("seq", "wshard"), None),
            P(("dp", "wshard"), None),
            P(("dp", "wshard")),
            P(("dp", "wshard")),
            P(("dp", "wshard"), None),
            P(("dp", "wshard")),
            P(("dp", "wshard")),
            P(("dp", "wshard")),
            P(("dp", "wshard"), None),
            P(("dp", "wshard")),
            P(("dp", "wshard"), None),
            P(("dp", "wshard")),
            P(("dp", "wshard")),
            P(("dp", "wshard")),
        ),
        check_vma=False,
    )
```

profile of v0, /device:TPU:1, one launch (start us, length us, event | category | flops | bytes accessed | tf_op | source)
XLA Modules:
  0.0 1603.3 jit_solution(16570990712837311823)
XLA Ops:
  8.0 20.7 %all-gather.1 = bf16[8,1,128]{2,1,0:T(2,128)(2,1)S(1)} all-gather(bf16[1,1,128]{2,1,0:T(2,128)(2,1)} %bitcast.337), channel_id=1, replica_groups=mesh['dp'=4,'seq'=16,'wshard'=2] {'dp','wshard'}, dimensions={0}, use_global_device_ids=true | all-gather | bytes 2304 | tf_op jit(solution)/shard_map/all_gather | solution.py:160
  28.7 14.8 all-gather
  43.6 58.4 %all-gather.15.cloned.1.call-done = bf16[1024,3072]{1,0:T(8,128)(2,1)} async-done(((bf16[128,3072]{1,0:T(8,128)(2,1)}), bf16[1024,3072]{1,0:T(8,128)(2,1)}) %all-gather.15.cloned.1.call-update) | async-done | bytes 6291472 | tf_op jit(solution)/shard_map/all_gather | solution.py:158
  102.0 8.7 copy.121
  117.5 26.4 %all_to_all.63 = bf16[2,128,3,1024]{1,0,2,3:T(2,128)(2,1)S(1)} all-to-all(bf16[2,128,3,1024]{1,0,2,3:T(2,128)(2,1)S(1)} %copy.122), channel_id=1, replica_groups=mesh['dp'=4,'seq'=16,'wshard'=2] {'seq'}, dimensions={3} | all-to-all | bytes 3145728 | tf_op jit(solution)/shard_map/all_to_all | solution.py:197
  147.5 63.1 %all_gather.54 = s32[2,4096]{1,0:T(2,128)S(1)} all-gather(s32[2,128]{1,0:T(2,128)S(1)} %copy-done.38), channel_id=1, replica_groups=mesh['dp'=4,'seq'=16,'wshard'=2] {'seq','wshard'}, dimensions={1}, use_global_device_ids=true | all-gather | bytes 33792 | tf_op jit(solution)/shard_map/all_gather | solution.py:205
  214.7 45.9 %while.54 = (s32[]{:T(128)}, bf16[2,2048,1,64]{1,3,2,0:T(8,128)(2,1)S(1)}, f32[2,4,1,512,1]{3,4,2,1,0:T(1,128)S(1)}, bf16[2,2048,1,64]{1,3,2,0:T(8,128)(2,1)}, s...) while((s32[]{:T(128)}, ...), condition=%wide.region_5.6_spmd, body=%wide.region_0.5_spmd.sunk | while | flops 555777536 | bytes 31713600 | solution.py:211
  217.3 19.9 %while.57 = (s32[]{:T(128)}, bf16[4,512,1,64]{1,3,2,0:T(8,128)(2,1)S(1)}, f32[4,1,512,1]{2,3,1,0:T(1,128)S(1)}, s32[4,512]{1,0:T(4,128)S(1)}, s32[4096]{0:T(1024...) while((s32[]{:T(128)}, ...), condition=%wide.region_4.4_spmd, body=%wide.region_1.3_spmd.sunk | while | flops 555777536 | bytes 26388588 | solution.py:90
  240.3 19.9 %while.57 = (s32[]{:T(128)}, bf16[4,512,1,64]{1,3,2,0:T(8,128)(2,1)S(1)}, f32[4,1,512,1]{2,3,1,0:T(1,128)S(1)}, s32[4,512]{1,0:T(4,128)S(1)}, s32[4096]{0:T(1024...) while((s32[]{:T(128)}, ...), condition=%wide.region_4.4_spmd, body=%wide.region_1.3_spmd.sunk | while | flops 555777536 | bytes 26388588 | solution.py:90
  268.6 103.6 %psum.106 = f32[]{:T(128)} all-reduce(f32[]{:T(128)} %convert_reduce_fusion), channel_id=1, replica_groups=mesh['dp'=4,'seq'=16,'wshard'=2] {'dp','seq','wshard'}, use_global_device_ids=true, to_apply=%region_13.14 | all-reduce | flops 1 | bytes 8 | tf_op jit(solution)/shard_map/psum | solution.py:238
  372.2 15.6 all-gather.2
  387.8 16.4 %all-gather.3 = bf16[8,1,128]{2,1,0:T(2,128)(2,1)S(1)} all-gather(bf16[1,1,128]{2,1,0:T(2,128)(2,1)S(1)} %bitcast.340), channel_id=1, replica_groups=mesh['dp'=4,'seq'=16,'wshard'=2] {'dp','wshard'}, dimensions={0}, use_global_device_ids=true | all-gather | bytes 2304 | tf_op jit(solution)/shard_map/all_gather | solution.py:163
  404.2 16.4 %all-gather.4 = bf16[8,1,128]{2,1,0:T(2,128)(2,1)S(1)} all-gather(bf16[1,1,128]{2,1,0:T(2,128)(2,1)S(1)} %bitcast.341), channel_id=1, replica_groups=mesh['dp'=4,'seq'=16,'wshard'=2] {'dp','wshard'}, dimensions={0}, use_global_device_ids=true | all-gather | bytes 2304 | tf_op jit(solution)/shard_map/all_gather | solution.py:164
  420.7 25.9 %all-gather.5 = bf16[8,1,512]{2,1,0:T(2,128)(2,1)S(1)} all-gather(bf16[1,1,512]{2,1,0:T(2,128)(2,1)S(1)} %reshape.289), channel_id=1, replica_groups=mesh['dp'=4,'seq'=16,'wshard'=2] {'dp','wshard'}, dimensions={0}, use_global_device_ids=true | all-gather | bytes 9216 | tf_op jit(solution)/shard_map/all_gather | solution.py:166
  446.6 16.3 %all-gather.6 = bf16[8,1,128]{2,1,0:T(2,128)(2,1)S(1)} all-gather(bf16[1,1,128]{2,1,0:T(2,128)(2,1)S(1)} %bitcast.342), channel_id=1, replica_groups=mesh['dp'=4,'seq'=16,'wshard'=2] {'dp','wshard'}, dimensions={0}, use_global_device_ids=true | all-gather | bytes 2304 | tf_op jit(solution)/shard_map/all_gather | solution.py:168
  463.6 15.7 all-gather.7
  479.3 16.6 %all-gather.8 = bf16[8,1,128]{2,1,0:T(2,128)(2,1)S(1)} all-gather(bf16[1,1,128]{2,1,0:T(2,128)(2,1)S(1)} %bitcast.344), channel_id=1, replica_groups=mesh['dp'=4,'seq'=16,'wshard'=2] {'dp','wshard'}, dimensions={0}, use_global_device_ids=true | all-gather | bytes 2304 | tf_op jit(solution)/shard_map/all_gather | solution.py:170
  500.3 7.8 convolution_add_fusion
  508.1 7.7 fusion.61
  532.1 32.6 %all-to-all-start.2 = ((bf16[2,128,1024]{1,0,2:T(2,128)(2,1)}), bf16[2,128,1024]{1,0,2:T(2,128)(2,1)S(1)}, u32[]{:S(2)}, u32[]{:S(2)}) async-start(bf16[2,128,1024]{1,0,2:T(2,128)(2,1)} %copy.129), calls=%async_computation.2 | async-start | bytes 1048576 | tf_op jit(solution)/shard_map/all_to_all | solution.py:279
  564.8 9.8 all-to-all-done.2
  576.1 235.6 %while.56 = (s32[]{:T(128)}, bf16[2,2048,1,64]{1,3,2,0:T(8,128)(2,1)}, bf16[2,4096,1,64]{1,3,2,0:T(8,128)(2,1)}, bf16[2,4096,1,64]{1,3,2,0:T(8,128)(2,1)}, bf16[...) while((s32[]{:T(128)}, ...), condition=%wide.region_22.23_spmd, body=%wide.region_18.22_spmd.sunk | while | flops 1366326784 | bytes 152489040 | solution.py:282
  580.9 110.8 %while.58 = (s32[]{:T(128)}, f32[4096,1,64]{0,2,1:T(8,128)S(1)}, f32[4096,1,64]{0,2,1:T(8,128)S(1)}, bf16[4,512,1,64]{1,3,2,0:T(8,128)(2,1)}, bf16[4,512,1,64]{1...) while((s32[]{:T(128)}, f32[4096,1,64]{0,2,1:T(8,128)S(1)}, ...), condition=%wide.region_21.21_spmd.clone, body=%wide.region_19.20_spmd.clone.sunk | while | flops 1366326784 | bytes 136152784 | solution.py:119
  588.8 10.1 multiply_convert_fusion.5
  616.5 10.1 multiply_convert_fusion.5
  644.2 10.1 multiply_convert_fusion.5
  671.9 10.1 multiply_convert_fusion.5
  698.6 110.8 %while.58 = (s32[]{:T(128)}, f32[4096,1,64]{0,2,1:T(8,128)S(1)}, f32[4096,1,64]{0,2,1:T(8,128)S(1)}, bf16[4,512,1,64]{1,3,2,0:T(8,128)(2,1)}, bf16[4,512,1,64]{1...) while((s32[]{:T(128)}, f32[4096,1,64]{0,2,1:T(8,128)S(1)}, ...), condition=%wide.region_21.21_spmd.clone, body=%wide.region_19.20_spmd.clone.sunk | while | flops 1366326784 | bytes 136152784 | solution.py:119
  706.5 10.1 multiply_convert_fusion.5
  734.2 10.1 multiply_convert_fusion.5
  761.9 10.1 multiply_convert_fusion.5
  789.5 10.1 multiply_convert_fusion.5
  811.6 9.8 copy.133
  828.7 13.3 pad_maximum_fusion
  845.6 110.6 %all-reduce.16.cloned.1.call-done = bf16[2,4096,2,64]{3,2,0,1:T(2,128)(2,1)} async-done(((bf16[2,4096,2,64]{3,2,0,1:T(2,128)(2,1)}), bf16[2,4096,2,64]{3,2,0,1:T(2,128)(2,1)}) %all-reduce.16.cloned.1.call-update) | async-done | bytes 2097168
  965.0 14.1 copy.169
  982.3 26.1 %all_to_all.64 = bf16[16,2,24576]{2,1,0:T(2,128)(2,1)S(1)} all-to-all(bf16[16,2,24576]{2,1,0:T(2,128)(2,1)} %reshape.343), channel_id=1, replica_groups=mesh['dp'=4,'seq'=16,'wshard'=2] {'seq'}, dimensions={0} | all-to-all | bytes 3145728 | tf_op jit(solution)/shard_map/all_to_all | solution.py:297
  1011.8 7.3 copy.137
  1023.6 8.6 copy.140
  1036.6 7.3 convolution_convert_fusion.2
  1045.2 8.4 convolution_convert_fusion.1
  1054.1 74.5 %reduce-scatter.13.cloned.1.call-done = bf16[128,3072]{1,0:T(8,128)(2,1)} async-done(((bf16[1024,3072]{1,0:T(8,128)(2,1)}), bf16[128,3072]{1,0:T(8,128)(2,1)}) %reduce-scatter.13.cloned.1.call-update) | async-done | bytes 786448
  1130.8 74.9 %reduce-scatter.7.cloned.1.call-done = bf16[128,1024]{1,0:T(8,128)(2,1)} async-done(((bf16[1024,1024]{1,0:T(8,128)(2,1)}), bf16[128,1024]{1,0:T(8,128)(2,1)}) %reduce-scatter.7.cloned.1.call-update) | async-done | bytes 262160 | tf_op jit(solution)/shard_map/reduce_scatter | solution.py:314
  1205.7 118.5 %reduce-scatter.9.cloned.1.call-done = bf16[128,4096]{1,0:T(8,128)(2,1)} async-done(((bf16[1024,4096]{1,0:T(8,128)(2,1)}), bf16[128,4096]{1,0:T(8,128)(2,1)}) %reduce-scatter.9.cloned.1.call-update) | async-done | bytes 1048592 | tf_op jit(solution)/shard_map/reduce_scatter | solution.py:326
  1324.2 116.0 %reduce-scatter.11.cloned.1.call-done = bf16[512,1024]{1,0:T(8,128)(2,1)} async-done(((bf16[4096,1024]{1,0:T(8,128)(2,1)}), bf16[512,1024]{1,0:T(8,128)(2,1)}) %reduce-scatter.11.cloned.1.call-update) | async-done | bytes 1048592 | tf_op jit(solution)/shard_map/reduce_scatter | solution.py:332
  1442.8 65.9 %psum.105 = f32[]{:T(128)} all-reduce(f32[]{:T(128)} %get-tuple-element.501), channel_id=1, replica_groups=mesh['dp'=4,'seq'=16,'wshard'=2] {'dp','seq','wshard'}, use_global_device_ids=true, to_apply=%region_11.12 | all-reduce | flops 1 | bytes 8 | tf_op jit(solution)/shard_map/psum | solution.py:238
  1510.0 31.6 %all-reduce.12 = (bf16[1024]{0:T(1024)(128)(2,1)S(1)}, bf16[1024]{0:T(1024)(128)(2,1)S(1)}, bf16[1024]{0:T(1024)(128)(2,1)S(1)}, bf16[1024]{0:T(1024)(128)(2,1)S...) all-reduce(bf16[1024]{0:T(1024)(128)(2,1)S(1)} %get-tuple-element.5, ...), channel_id=4, replica_groups=mesh['dp'=4,'seq'=16,'wshard'=2] {'dp','wshard'}, use_global_device_ids=true, to_apply=%region_27.28.clone | all-reduce | flops 12288 | bytes 49152
  1542.3 34.7 %all-reduce.10 = (bf16[128]{0:T(256)(128)(2,1)S(1)}, bf16[128]{0:T(256)(128)(2,1)S(1)}, bf16[128]{0:T(256)(128)(2,1)S(1)}, bf16[128]{0:T(256)(128)(2,1)S(1)}, bf...) all-reduce(bf16[128]{0:T(256)(128)(2,1)S(1)} %dynamic-slice.3, ...), channel_id=1, replica_groups=mesh['dp'=4,'seq'=16,'wshard'=2] {'seq'}, use_global_device_ids=true, to_apply=%region_28.29 | all-reduce | flops 1536 | bytes 6144 | tf_op jit(solution)/shard_map/psum | solution.py:347
  (432 shorter events, 302.7 us)
Async XLA Ops:
  7.2 94.8 %all-gather.15.cloned.1.call-start = ((), (), s32[]{:S(2)}) async-start(), calls=%async_computation.8 | async-start | bytes 7077888 | tf_op jit(solution)/shard_map/all_gather | solution.py:158
  7.9 203.6 %all-gather.17.cloned.1.call-start = ((), (), s32[]{:S(2)}) async-start(), calls=%async_computation.9 | async-start | bytes 3145728 | tf_op jit(solution)/shard_map/all_gather | solution.py:201
  102.0 8.7 copy-start.13
  145.6 351.7 %all-gather.19.cloned.1.call-start = ((), (), s32[]{:S(2)}) async-start(), calls=%async_computation.10 | async-start | bytes 2359296 | tf_op jit(solution)/shard_map/all_gather | solution.py:161
  146.3 353.9 %all-gather.21.cloned.1.call-start = ((), (), s32[]{:S(2)}) async-start(), calls=%async_computation.11 | async-start | bytes 9437184 | tf_op jit(solution)/shard_map/all_gather | solution.py:165
  146.9 361.1 %all-gather.23.cloned.1.call-start = ((), (), s32[]{:S(2)}) async-start(), calls=%async_computation.12 | async-start | bytes 9437184 | tf_op jit(solution)/shard_map/all_gather | solution.py:167
  260.6 111.6 %copy-start.41 = (bf16[128]{0:T(256)(128)(2,1)S(1)}, bf16[128]{0:T(256)(128)(2,1)}, u32[]{:S(2)}) copy-start(bf16[128]{0:T(256)(128)(2,1)} %param.33) | copy-start | bytes 772
  260.6 127.1 %copy-start.42 = (bf16[128]{0:T(256)(128)(2,1)S(1)}, bf16[128]{0:T(256)(128)(2,1)}, u32[]{:S(2)}) copy-start(bf16[128]{0:T(256)(128)(2,1)} %param.34) | copy-start | bytes 772
  260.7 143.6 %copy-start.43 = (bf16[128]{0:T(256)(128)(2,1)S(1)}, bf16[128]{0:T(256)(128)(2,1)}, u32[]{:S(2)}) copy-start(bf16[128]{0:T(256)(128)(2,1)} %param.35) | copy-start | bytes 772
  260.7 160.0 %copy-start.39 = (bf16[512]{0:T(512)(128)(2,1)S(1)}, bf16[512]{0:T(512)(128)(2,1)}, u32[]{:S(2)}) copy-start(bf16[512]{0:T(512)(128)(2,1)} %param.37) | copy-start | bytes 3076
  260.7 185.9 %copy-start.44 = (bf16[128]{0:T(256)(128)(2,1)S(1)}, bf16[128]{0:T(256)(128)(2,1)}, u32[]{:S(2)}) copy-start(bf16[128]{0:T(256)(128)(2,1)} %param.39) | copy-start | bytes 772
  260.7 202.9 %copy-start.45 = (bf16[128]{0:T(256)(128)(2,1)S(1)}, bf16[128]{0:T(256)(128)(2,1)}, u32[]{:S(2)}) copy-start(bf16[128]{0:T(256)(128)(2,1)} %param.40) | copy-start | bytes 772
  260.7 218.6 %copy-start.46 = (bf16[128]{0:T(256)(128)(2,1)S(1)}, bf16[128]{0:T(256)(128)(2,1)}, u32[]{:S(2)}) copy-start(bf16[128]{0:T(256)(128)(2,1)} %param.41) | copy-start | bytes 772
  260.7 236.6 %copy-start.14 = (bf16[2,128,1024]{2,1,0:T(8,128)(2,1)S(1)}, bf16[2,128,1024]{2,1,0:T(8,128)(2,1)}, u32[]{:S(2)}) copy-start(bf16[2,128,1024]{2,1,0:T(8,128)(2,1)} %param.25) | copy-start | bytes 1572868
  263.0 232.9 %all-to-all-start.1 = ((bf16[16,2,8192]{2,1,0:T(2,128)(2,1)}), bf16[16,2,8192]{2,1,0:T(2,128)(2,1)S(1)}, u32[]{:S(2)}, u32[]{:S(2)}) async-start(bf16[16,2,8192]{2,1,0:T(2,128)(2,1)} %reshape.341), calls=%async_computation.1 | async-start | bytes 1048576 | tf_op jit(solution)/shard_map/all_to_all | solution.py:214
  404.2 124.0 %copy-start.23 = (f32[8,1,128]{2,1,0:T(1,128)}, f32[8,1,128]{2,1,0:T(1,128)S(1)}, u32[]{:S(2)}) copy-start(f32[8,1,128]{2,1,0:T(1,128)S(1)} %convert_element_type.252) | copy-start | bytes 12292
  420.6 87.4 %copy-start.25 = (f32[8,1,128]{2,1,0:T(1,128)}, f32[8,1,128]{2,1,0:T(1,128)S(1)}, u32[]{:S(2)}) copy-start(f32[8,1,128]{2,1,0:T(1,128)S(1)} %convert_element_type.253) | copy-start | bytes 12292
  497.3 10.8 copy-start.10
  499.9 28.3 %copy-start.2 = (f32[256,1024]{1,0:T(8,128)}, f32[256,1024]{1,0:T(8,128)S(1)}, u32[]{:S(2)}) copy-start(f32[256,1024]{1,0:T(8,128)S(1)} %get-tuple-element.621) | copy-start | bytes 3145732
  499.9 28.3 %copy-start.27 = (f32[256]{0:T(256)}, f32[256]{0:T(256)S(1)}, u32[]{:S(2)}) copy-start(f32[256]{0:T(256)S(1)} %broadcast_multiply_fusion.5) | copy-start | bytes 3076
  500.2 28.0 %copy-start.29 = (f32[256]{0:T(256)}, f32[256]{0:T(256)S(1)}, u32[]{:S(2)}) copy-start(f32[256]{0:T(256)S(1)} %add_rsqrt_fusion.1) | copy-start | bytes 3076
  508.1 11.4 slice-start.2
  508.1 8.0 copy-start.17
  508.1 11.4 slice-start.3
  532.1 42.5 %all-to-all-start.2 = ((bf16[2,128,1024]{1,0,2:T(2,128)(2,1)}), bf16[2,128,1024]{1,0,2:T(2,128)(2,1)S(1)}, u32[]{:S(2)}, u32[]{:S(2)}) async-start(bf16[2,128,1024]{1,0,2:T(2,128)(2,1)} %copy.129), calls=%async_computation.2 | async-start | bytes 1048576 | tf_op jit(solution)/shard_map/all_to_all | solution.py:279
  564.7 391.5 %all-reduce.16.cloned.1.call-start = ((), (), s32[]{:S(2)}) async-start(), calls=%async_computation.17 | async-start | bytes 8388608
  598.9 7.9 copy-start
  654.3 7.9 copy-start
  682.0 7.9 copy-start
  716.6 7.9 copy-start
  772.0 7.9 copy-start
  799.7 7.9 copy-start
  811.6 9.8 copy-start.18
  842.0 286.5 %reduce-scatter.13.cloned.1.call-start = ((), (), s32[]{:S(2)}) async-start(), calls=%async_computation.16 | async-start | bytes 7077888
  1008.4 10.7 copy-start.15
  1032.3 173.4 %reduce-scatter.7.cloned.1.call-start = ((), (), s32[]{:S(2)}) async-start(), calls=%async_computation.13 | async-start | bytes 2359296 | tf_op jit(solution)/shard_map/reduce_scatter | solution.py:314
  1036.5 287.7 %reduce-scatter.9.cloned.1.call-start = ((), (), s32[]{:S(2)}) async-start(), calls=%async_computation.14 | async-start | bytes 9437184 | tf_op jit(solution)/shard_map/reduce_scatter | solution.py:326
  1044.0 396.2 %reduce-scatter.11.cloned.1.call-start = ((), (), s32[]{:S(2)}) async-start(), calls=%async_computation.15 | async-start | bytes 9437184 | tf_op jit(solution)/shard_map/reduce_scatter | solution.py:332
  1053.7 386.6 %copy-start.47 = (u32[128]{0:T(128)S(1)}, u32[128]{0:T(128)}, u32[]{:S(2)}) copy-start(u32[128]{0:T(128)} %constant.146) | copy-start | bytes 1540
  1053.7 456.3 %copy-start.31 = (bf16[1024]{0:T(1024)(128)(2,1)S(1)}, bf16[1024]{0:T(1024)(128)(2,1)}, u32[]{:S(2)}) copy-start(bf16[1024]{0:T(1024)(128)(2,1)} %get-tuple-element.498) | copy-start | bytes 6148
  1053.7 456.3 %copy-start.32 = (bf16[1024]{0:T(1024)(128)(2,1)S(1)}, bf16[1024]{0:T(1024)(128)(2,1)}, u32[]{:S(2)}) copy-start(bf16[1024]{0:T(1024)(128)(2,1)} %get-tuple-element.499) | copy-start | bytes 6148
  1053.7 456.3 %copy-start.33 = (bf16[1024]{0:T(1024)(128)(2,1)S(1)}, bf16[1024]{0:T(1024)(128)(2,1)}, u32[]{:S(2)}) copy-start(bf16[1024]{0:T(1024)(128)(2,1)} %get-tuple-element.605) | copy-start | bytes 6148
  1053.7 456.3 %copy-start.34 = (bf16[4096]{0:T(1024)(128)(2,1)S(1)}, bf16[4096]{0:T(1024)(128)(2,1)}, u32[]{:S(2)}) copy-start(bf16[4096]{0:T(1024)(128)(2,1)} %get-tuple-element.625) | copy-start | bytes 24580
  1053.7 456.3 %copy-start.35 = (bf16[1024]{0:T(1024)(128)(2,1)S(1)}, bf16[1024]{0:T(1024)(128)(2,1)}, u32[]{:S(2)}) copy-start(bf16[1024]{0:T(1024)(128)(2,1)} %get-tuple-element.607) | copy-start | bytes 6148
  1053.7 456.3 %copy-start.36 = (bf16[1024]{0:T(1024)(128)(2,1)S(1)}, bf16[1024]{0:T(1024)(128)(2,1)}, u32[]{:S(2)}) copy-start(bf16[1024]{0:T(1024)(128)(2,1)} %get-tuple-element.496) | copy-start | bytes 6148
  1053.7 456.3 %copy-start.37 = (bf16[1024]{0:T(1024)(128)(2,1)S(1)}, bf16[1024]{0:T(1024)(128)(2,1)}, u32[]{:S(2)}) copy-start(bf16[1024]{0:T(1024)(128)(2,1)} %get-tuple-element.506) | copy-start | bytes 6148
  1053.7 528.0 %copy-start.5 = (f32[256,1024]{1,0:T(8,128)S(1)}, f32[256,1024]{1,0:T(8,128)}, u32[]{:S(2)}) copy-start(f32[256,1024]{1,0:T(8,128)} %copy-done.4) | copy-start | bytes 3145732
  1053.7 533.6 %all-reduce.18.cloned.1.call-start = ((), (), s32[]{:S(2)}) async-start(), calls=%async_computation.18 | async-start | bytes 6291456 | tf_op jit(solution)/shard_map/psum | solution.py:346
  (36 other events, 156.2 us)
Sparse Core Ops, SparseCore 0:
  10.3 91.6 all-gather.14
  145.7 34.3 all-gather.16
  182.5 52.8 all-gather.18
  237.5 105.8 all-gather.20
  345.6 105.2 all-gather.22
  842.1 114.0 all-reduce.15
  1032.4 96.0 reduce-scatter.12
  1133.3 72.4 reduce-scatter.6
  1210.0 114.1 reduce-scatter.8
  1327.9 112.2 reduce-scatter.10
  1443.8 128.5 all-reduce.17
where the time goes:
time: 1610 us; the launch traced here: 1600 us
  waiting for transfers between devices  565 us (35%)
  blocking collectives  510 us (32%)
  matrix products  229 us (14%)
  other arithmetic  127 us (8%)
  local copies, waits for them, and re-layouts  112 us (7%)
  starting transfers between devices  38.3 us (2%)
  between operations  20.3 us (1%)
    unnamed x13, waiting for transfers between devices  188 us
    psum x2, blocking collectives, on_device(): lax.psum((jnp.sum(valid_col * differ * differ), jnp.sum(valid_col)), ('dp...  170 us
    reduce_scatter x1, waiting for transfers between devices, on_device(): lax.psum_scatter(grad_up.astype(jnp.bfloat16), ('dp', 'wshard'), scatter_...  119 us
    reduce_scatter x1, waiting for transfers between devices, on_device(): lax.psum_scatter(grad_down.astype(jnp.bfloat16), ('dp', 'wshard'), scatte...  116 us
    convert_element_type x8, other arithmetic, attend_back(): (1.0 / math.sqrt(HD) * (probs * (grad_probs - row_dot))).astype(jnp.bfloa...  80.8 us
    reduce_scatter x1, waiting for transfers between devices, on_device(): lax.psum_scatter(grad_out.astype(jnp.bfloat16), ('dp', 'wshard'), scatter...  74.9 us
    all_gather x1, blocking collectives, on_device(): lax.all_gather(segments, ('seq', 'wshard'), axis=1, tiled=True)  63.1 us
    all_gather x1, waiting for transfers between devices, on_device(): lax.all_gather(w_qkv, ('dp', 'wshard'), axis=0, tiled=True)  58.4 us
  transfers between devices with their start and end apart: 13, of which 7 were waited for; matrix products, arithmetic and copies ran while one was open for 6% of the time, Pallas kernels for 0%

commit v1 on v0

v1 whole, which is shorter than its diff:
```python
import functools

import jax
import jax.numpy as jnp
from jax import lax
from jax.experimental import pallas as pl
from jax.experimental.pallas import tpu as pltpu
from jax.sharding import PartitionSpec as P

D = 1024
H = 16
HD = 64
FF = 4096
L = 4096
EPS = 1e-06
F32 = jnp.float32
BF = jnp.bfloat16
MASKED = 1000000000.0
VMEM_CAP = 60 * 1024 * 1024
MESH = pl.DeviceIdType.MESH
ANY = pl.BlockSpec(memory_space=pl.ANY)
TB = 128
NB = L // TB


def dot(first, second, dims=((1,), (0,))):
    return lax.dot_general(first, second, (dims, ((), ())), preferred_element_type=F32)


def project_kernel(
    x_ref, heads_ref, smalls_ref, meta_ref, qat_ref, ka_ref, vat_ref, va_ref, kt_ref, q_ref, w_ref, wt_ref, b_ref
):
    _, _, _, core = place()

    @pl.when(pl.program_id(0) == 0)
    def _():
        pair = lax.axis_index("seq") // 2
        first = core == 0
        both = heads_ref[...]
        own = [jnp.where(first, both[:, 128 * p : 128 * p + HD], both[:, 128 * p + HD : 128 * (p + 1)]) for p in range(3)]
        w_ref[...] = jnp.concatenate(own, axis=1)
        wt_ref[...] = w_ref[...].astype(F32).T.astype(BF)
        mine = smalls_ref[pair]
        bias = [jnp.where(first, mine[k : k + 1, :HD], mine[k : k + 1, HD:]) for k in range(2)]
        b_ref[...] = jnp.broadcast_to(jnp.concatenate([bias[0], jnp.zeros((1, HD), F32), bias[1]], axis=1), (8, 3 * HD))

    x = x_ref[...]
    rows = x.shape[0]
    side = dot(x, w_ref[...]) + b_ref[:1, :]
    turned = dot(wt_ref[...], x, ((1,), (1,))) + b_ref[...].T[:, :1]
    q8 = (side[:, :HD].astype(BF).astype(F32) * 0.125).astype(BF)
    q8t = (turned[:HD].astype(BF).astype(F32) * 0.125).astype(BF)
    k = side[:, HD : 2 * HD].astype(BF)
    v = side[:, 2 * HD :].astype(BF)
    segment = jnp.concatenate([meta_ref[i, 0:1, :] for i in range(rows // TB)], axis=1)
    hot = jnp.where(lax.broadcasted_iota(jnp.int32, (32, rows), 0) == segment, 1.0, 0.0)
    apart = (hot.T - 1.0) * MASKED
    lane = lax.broadcasted_iota(jnp.int32, (rows, 32), 1)
    ones3 = jnp.where(lane < 3, 1.0, 0.0)
    zero_side = jnp.zeros((rows, 32), F32)
    q_ref[...] = q8
    qat_ref[...] = jnp.concatenate([q8t, hot.astype(BF), jnp.zeros((32, rows), BF)], axis=0)
    ka_ref[...] = jnp.concatenate([k, apart.astype(BF), ones3.astype(BF)], axis=1)
    va_ref[...] = jnp.concatenate([v, ones3.astype(BF), zero_side.astype(BF)], axis=1)
    kt_ref[...] = turned[HD : 2 * HD].astype(BF)
    ones_row = jnp.where(lax.broadcasted_iota(jnp.int32, (16, rows), 0) == 0, 1.0, 0.0)
    vat_ref[...] = jnp.concatenate([turned[2 * HD :].astype(BF), ones_row.astype(BF)], axis=0)


def project(x, heads, smalls, meta, rows=1024):
    return pl.pallas_call(
        project_kernel,
        grid=(L // rows,),
        in_specs=[
            pl.BlockSpec((rows, D), lambda i: (i, 0)),
            pl.BlockSpec((D, 384), lambda i: (0, 0)),
            pl.BlockSpec((8, 16, 128), lambda i: (0, 0, 0)),
            pl.BlockSpec((rows // TB, 8, TB), lambda i: (i, 0, 0)),
        ],
        out_specs=[
            pl.BlockSpec((128, rows), lambda i: (0, i)),
            pl.BlockSpec((rows, 128), lambda i: (i, 0)),
            pl.BlockSpec((80, rows), lambda i: (0, i)),
            pl.BlockSpec((rows, 128), lambda i: (i, 0)),
            pl.BlockSpec((HD, rows), lambda i: (0, i)),
            pl.BlockSpec((rows, HD), lambda i: (i, 0)),
        ],
        out_shape=[
            jax.ShapeDtypeStruct((128, L), BF),
            jax.ShapeDtypeStruct((L, 128), BF),
            jax.ShapeDtypeStruct((80, L), BF),
            jax.ShapeDtypeStruct((L, 128), BF),
            jax.ShapeDtypeStruct((HD, L), BF),
            jax.ShapeDtypeStruct((L, HD), BF),
        ],
        scratch_shapes=[pltpu.VMEM((D, 3 * HD), BF), pltpu.VMEM((3 * HD, D), BF), pltpu.VMEM((8, 3 * HD), F32)],
        name="project_head",
        compiler_params=pltpu.CompilerParams(vmem_limit_bytes=VMEM_CAP),
    )(x, heads, smalls, meta)


def attend_kernel(key_rows, qat_ref, ka_ref, vat_ref, blocks_ref, wide_ref, lse_ref):
    queries = qat_ref[...]
    width = queries.shape[1]
    peak = jnp.full((1, width), -jnp.inf, F32)
    total = jnp.zeros((80, width), F32)
    for j in range(L // key_rows):
        rows = slice(j * key_rows, (j + 1) * key_rows)
        logits = dot(ka_ref[rows, :], queries)
        new_peak = jnp.maximum(peak, jnp.max(logits, axis=0, keepdims=True))
        expos = jnp.exp(logits - new_peak).astype(BF)
        total = total * jnp.exp(peak - new_peak) + dot(vat_ref[:, rows], expos)
        peak = new_peak
    sums = total[HD : HD + 1]
    context = total[:HD] / sums
    wide_ref[...] = context
    lse_ref[...] = peak + jnp.log(sums)
    low = context.astype(BF)
    for j in range(width // TB):
        blocks_ref[j] = low[:, j * TB : (j + 1) * TB]


def attend(qat, ka, vat, width=1024, key_rows=512):
    return pl.pallas_call(
        functools.partial(attend_kernel, key_rows),
        grid=(L // width,),
        in_specs=[
            pl.BlockSpec((128, width), lambda i: (0, i)),
            pl.BlockSpec((L, 128), lambda i: (0, 0)),
            pl.BlockSpec((80, L), lambda i: (0, 0)),
        ],
        out_specs=[
            pl.BlockSpec((width // TB, HD, TB), lambda i: (i, 0, 0)),
            pl.BlockSpec((HD, width), lambda i: (0, i)),
            pl.BlockSpec((1, width), lambda i: (0, i)),
        ],
        out_shape=[
            jax.ShapeDtypeStruct((NB, HD, TB), BF),
            jax.ShapeDtypeStruct((HD, L), F32),
            jax.ShapeDtypeStruct((1, L), F32),
        ],
        name="attend",
        compiler_params=pltpu.CompilerParams(vmem_limit_bytes=VMEM_CAP),
    )(qat, ka, vat)


def three_pieces(row):
    high = row.astype(BF)
    rest = row - high.astype(F32)
    middle = rest.astype(BF)
    lowest = (rest - middle.astype(F32)).astype(BF)
    return jnp.concatenate([high, middle, lowest], axis=0)


def attend_back_kernel(
    key_rows, qat_ref, ka_ref, va_ref, kt_ref, q_ref, do_ref, wide_ref, lse_ref, dqkv_ref, dk_ref, dv_ref
):
    step = pl.program_id(0)

    @pl.when(step == 0)
    def _():
        dk_ref[...] = jnp.zeros_like(dk_ref)
        dv_ref[...] = jnp.zeros_like(dv_ref)

    width = qat_ref.shape[1]
    grad_t = jnp.concatenate([do_ref[j] for j in range(width // TB)], axis=1)
    delta = jnp.sum(grad_t.astype(F32) * wide_ref[...], axis=0, keepdims=True)
    queries = jnp.concatenate(
        [qat_ref[:96, :], three_pieces(-lse_ref[...]), jnp.zeros((29, width), BF)], axis=0
    )
    grads = jnp.concatenate([grad_t, three_pieces(-delta), jnp.zeros((61, width), BF)], axis=0)
    grad_rows = grad_t.astype(F32).T.astype(BF)
    query_rows = q_ref[...]
    dq = jnp.zeros((HD, width), F32)
    for j in range(L // key_rows):
        rows = slice(j * key_rows, (j + 1) * key_rows)
        probs = jnp.exp(dot(ka_ref[rows, :], queries))
        raw = (probs * dot(va_ref[rows, :], grads)).astype(BF)
        dv_ref[rows, :] += dot(probs.astype(BF), grad_rows)
        dk_ref[rows, :] += dot(raw, query_rows)
        dq = dq + dot(kt_ref[:, rows], raw)
    dq_low = (dq * 0.125).astype(BF)
    for j in range(width // TB):
        dqkv_ref[step * (width // TB) + j, 0:HD, :] = dq_low[:, j * TB : (j + 1) * TB]

    @pl.when(step == pl.num_programs(0) - 1)
    def _():
        for j in range(NB):
            rows = slice(j * TB, (j + 1) * TB)
            dqkv_ref[j, HD : 2 * HD, :] = dk_ref[rows, :].T.astype(BF)
            dqkv_ref[j, 2 * HD :, :] = dv_ref[rows, :].T.astype(BF)


def attend_back(qat, ka, va, kt, q8, do, wide, lse, width=1024, key_rows=512):
    def whole(shape):
        return pl.BlockSpec(shape, lambda i: (0,) * len(shape))

    return pl.pallas_call(
        functools.partial(attend_back_kernel, key_rows),
        grid=(L // width,),
        in_specs=[
            pl.BlockSpec((128, width), lambda i: (0, i)),
            whole((L, 128)),
            whole((L, 128)),
            whole((HD, L)),
            pl.BlockSpec((width, HD), lambda i: (i, 0)),
            pl.BlockSpec((width // TB, HD, TB), lambda i: (i, 0, 0)),
            pl.BlockSpec((HD, width), lambda i: (0, i)),
            pl.BlockSpec((1, width), lambda i: (0, i)),
        ],
        out_specs=whole((NB, 3 * HD, TB)),
        out_shape=jax.ShapeDtypeStruct((NB, 3 * HD, TB), BF),
        scratch_shapes=[pltpu.VMEM((L, HD), F32), pltpu.VMEM((L, HD), F32)],
        name="attend_back",
        compiler_params=pltpu.CompilerParams(vmem_limit_bytes=VMEM_CAP),
    )(qat, ka, va, kt, q8, do, wide, lse)


def place():
    at = lax.axis_index("seq")
    return (lax.axis_index("wshard") * 2 + (at // 2) % 2, lax.axis_index("dp"), at // 4, at % 2)


def device_at(x, y, z, core):
    return (y, (z * 2 + x % 2) * 2 + core, x // 2)


def along(axis, shift):
    x, y, z, core = place()
    if axis == "x":
        return device_at((x + shift) % 4, y, z, core)
    if axis == "y":
        return device_at(x, (y + shift) % 4, z, core)
    return device_at(x, y, (z + shift) % 4, core)


def sibling():
    x, y, z, core = place()
    return device_at(x, y, z, 1 - core)


def greet(partners):
    barrier = pltpu.get_barrier_semaphore()
    for partner in partners:
        pl.semaphore_signal(barrier, inc=1, device_id=partner, device_id_type=MESH)
    pl.semaphore_wait(barrier, len(partners))


def remote(src, dst, send_sem, recv_sem, target):
    return pltpu.make_async_remote_copy(
        src_ref=src, dst_ref=dst, send_sem=send_sem, recv_sem=recv_sem, device_id=target, device_id_type=MESH
    )


ORDERS = ("yzx", "zxy", "xyz")


def ring_partners():
    return [along(axis, shift) for axis in "xyz" for shift in (1, 2, 3)] + [sibling()]


def reduce_scratch():
    return [
        pltpu.VMEM((4, 2, 384, 512), BF),
        pltpu.VMEM((4, 4, 2, 96, 512), BF),
        pltpu.VMEM((4, 4, 192, 512), BF),
        pltpu.VMEM((4, 2, 96, 512), BF),
        pltpu.VMEM((4, 4, 48, 512), BF),
        pltpu.VMEM((4, 192, 512), BF),
        pltpu.VMEM((3, 4, 48, 512), BF),
        pltpu.SemaphoreType.DMA((3, 3, 3)),
        pltpu.SemaphoreType.DMA((3, 3, 3)),
        pltpu.SemaphoreType.DMA((3,)),
        pltpu.SemaphoreType.DMA((3, 8)),
        pltpu.SemaphoreType.DMA((3, 8)),
    ]


def aligned(value, unit):
    return pl.multiple_of(value, unit)


def reduce_pieces(stage, part, refs, at):
    g_ref, a1, b1, c1, a2, b2, c2, last = refs[:8]
    half, low = at // 2, at % 2
    if stage == 0:
        return (
            lambda: g_ref.at[at, :, pl.ds(0, 384), :],
            lambda: g_ref.at[:, :, pl.ds(aligned(384 + at * 96, 96), 96), :],
            lambda: g_ref.at[:, half, pl.ds(aligned(768 + low * 192, 192), 192), :],
        )[part]()
    if stage == 1:
        return (
            lambda: a1.at[0, :, pl.ds(aligned(at * 96, 96), 96), :],
            lambda: b1.at[0, :, half, pl.ds(aligned(low * 48, 48), 48), :],
            lambda: c1.at[0, at],
        )[part]()
    return (
        lambda: a2.at[0, half, pl.ds(aligned(low * 48, 48), 48), :],
        lambda: b2.at[0, at],
        lambda: c2.at[0, pl.ds(aligned(at * 48, 48), 48), :],
    )[part]()


def reduce_landing(stage, part, refs, slot):
    g_ref, a1, b1, c1, a2, b2, c2, last = refs[:8]
    if stage == 0:
        return (a1, b1, c1)[part].at[slot]
    if stage == 1:
        return (a2, b2, c2)[part].at[slot]
    return last.at[part, slot]


def ring_at(axis):
    x, y, z, _ = place()
    return {"x": x, "y": y, "z": z}[axis]


def reduce_copies(stage, refs):
    send, recv = refs[8], refs[9]
    copies = []
    for shift in (1, 2, 3):
        for part in range(3):
            axis = ORDERS[part][stage]
            target_at = (ring_at(axis) + shift) % 4
            copies.append(
                remote(
                    reduce_pieces(stage, part, refs, target_at),
                    reduce_landing(stage, part, refs, shift),
                    send.at[stage, part, shift - 1],
                    recv.at[stage, part, shift - 1],
                    along(axis, shift),
                )
            )
    return copies


def reduce_own(refs):
    return [
        pltpu.make_async_copy(
            reduce_pieces(0, part, refs, ring_at(ORDERS[part][0])), reduce_landing(0, part, refs, 0), refs[10].at[part]
        )
        for part in range(3)
    ]


def reduce_start(refs):
    for copy in reduce_copies(0, refs):
        copy.start()
    for copy in reduce_own(refs):
        copy.start()


def add_four(values):
    total = values[0].astype(F32) + values[1].astype(F32)
    return (total + values[2].astype(F32) + values[3].astype(F32)).astype(BF)


def reduce_step(stage, refs):
    g_ref, a1, b1, c1, a2, b2, c2, last = refs[:8]
    for copy in reduce_copies(stage, refs):
        copy.wait()
    x, y, z, _ = place()
    if stage == 0:
        for copy in reduce_own(refs):
            copy.wait()

        @pl.loop(0, 16)
        def _(i):
            k = aligned((i % 8) * 48, 48)
            a1[0, i // 8, pl.ds(k, 48), :] = add_four([a1[s, i // 8, pl.ds(k, 48), :] for s in range(4)])
            k = aligned((i % 2) * 48, 48)
            b1[0, i // 4, (i // 2) % 2, pl.ds(k, 48), :] = add_four(
                [b1[s, i // 4, (i // 2) % 2, pl.ds(k, 48), :] for s in range(4)]
            )
            k = aligned((i % 4) * 48, 48)
            c1[0, i // 4, pl.ds(k, 48), :] = add_four([c1[s, i // 4, pl.ds(k, 48), :] for s in range(4)])

    elif stage == 1:

        @pl.loop(0, 4)
        def _(i):
            k = aligned((i % 2) * 48, 48)
            own = a1[0, i // 2, pl.ds(aligned(z * 96 + (i % 2) * 48, 48), 48), :]
            a2[0, i // 2, pl.ds(k, 48), :] = add_four([own] + [a2[s, i // 2, pl.ds(k, 48), :] for s in (1, 2, 3)])
            own = b1[0, i, x // 2, pl.ds(aligned((x % 2) * 48, 48), 48), :]
            b2[0, i] = add_four([own] + [b2[s, i] for s in (1, 2, 3)])
            k = aligned(i * 48, 48)
            own = c1[0, y, pl.ds(k, 48), :]
            c2[0, pl.ds(k, 48), :] = add_four([own] + [c2[s, pl.ds(k, 48), :] for s in (1, 2, 3)])

    else:
        own = a2[0, x // 2, pl.ds(aligned((x % 2) * 48, 48), 48), :]
        last[0, 0] = add_four([own] + [last[0, s] for s in (1, 2, 3)])
        last[1, 0] = add_four([b2[0, y]] + [last[1, s] for s in (1, 2, 3)])
        own = c2[0, pl.ds(aligned(z * 48, 48), 48), :]
        last[2, 0] = add_four([own] + [last[2, s] for s in (1, 2, 3)])
    if stage < 2:
        for copy in reduce_copies(stage + 1, refs):
            copy.start()


def shard_rows(o_ref, part, x_low, z, core):
    sub = x_low * 4 + z if part == 2 else z * 2 + x_low
    return o_ref.at[core, pl.ds(aligned(part * 384 + sub * 48, 48), 48), :]


def spread(refs, o_ref):
    last, local = refs[7], refs[10]
    send, recv = refs[11], refs[12]
    x, y, z, core = place()
    low = x % 2
    pair = device_at(x // 2 * 2 + 1 - low, y, z, core)
    first, own, second, third = [], [], [], []
    for part in range(3):
        mine = last.at[part, 0]
        own.append(pltpu.make_async_copy(mine, shard_rows(o_ref, part, low, z, core), local.at[part]))
        first.append(remote(mine, shard_rows(o_ref, part, low, z, core), send.at[part, 0], recv.at[part, 0], pair))
        for shift in (1, 2, 3):
            place_there = shard_rows(o_ref, part, low, z, core)
            second.append(remote(mine, place_there, send.at[part, shift], recv.at[part, shift], along("z", shift)))
            place_there = shard_rows(o_ref, part, 1 - low, z, core)
            third.append(
                remote(place_there, place_there, send.at[part, 3 + shift], recv.at[part, 3 + shift], along("z", shift))
            )
    for copy in own + first + second:
        copy.start()
    for copy in first:
        copy.wait()
    for copy in third:
        copy.start()
    for copy in own + second + third:
        copy.wait()
    rows = o_ref.at[core]
    across = remote(rows, rows, send.at[0, 7], recv.at[0, 7], sibling())
    across.start()
    across.wait()


def swap_partner(shift):
    mine = lax.axis_index("seq") * 2 + lax.axis_index("wshard")
    other = (mine + shift) % NB
    return other, (lax.axis_index("dp"), other // 2, other % 2)


def swap_greet():
    barrier = pltpu.get_barrier_semaphore()

    @pl.loop(1, NB)
    def _(shift):
        pl.semaphore_signal(barrier, inc=1, device_id=swap_partner(shift)[1], device_id_type=MESH)

    pl.semaphore_wait(barrier, NB - 1)


def swap_copies(piece_for, landing_from, sems):
    mine = lax.axis_index("seq") * 2 + lax.axis_index("wshard")
    send, recv, local = sems

    def copy(shift):
        other, device = swap_partner(shift)
        return remote(piece_for(other), landing_from(mine), send.at[shift], recv.at[shift], device)

    own = pltpu.make_async_copy(piece_for(mine), landing_from(mine), local)

    def start():
        @pl.loop(1, NB)
        def _(shift):
            copy(shift).start()

        own.start()

    def wait():
        @pl.loop(1, NB)
        def _(shift):
            copy(shift).wait()

        own.wait()

    return start, wait


def swap_sems():
    return [pltpu.SemaphoreType.DMA((NB,)), pltpu.SemaphoreType.DMA((NB,)), pltpu.SemaphoreType.DMA]


def block_of(ref, b):
    return ref.at[b]


def head_tile(ref, b):
    return ref.at[pl.ds(aligned((b // 2) * HD, HD), HD), pl.ds(aligned((b % 2) * TB, TB), TB)]


def head_tile3(ref, b):
    return ref.at[:, pl.ds(aligned((b // 2) * HD, HD), HD), pl.ds(aligned((b % 2) * TB, TB), TB)]


HALVES = ((128, 2048), (256, 1024))


class Transfers:
    def __init__(self, send, recv):
        self.send, self.recv, self.used = send, recv, 0

    def copy(self, src, dst, target):
        made = remote(src, dst, self.send.at[self.used], self.recv.at[self.used], target)
        self.used += 1
        return made


def start_all(copies):
    for copy in copies:
        copy.start()


def wait_all(copies):
    for copy in copies:
        copy.wait()


def unit_rows(matrix, unit, count=1):
    rows = HALVES[matrix][0] // 4
    return pl.ds(unit * rows, count * rows)


def columns_part(matrix, at, parts):
    width = HALVES[matrix][1] // parts
    return pl.ds(aligned(at * width, 128), width)


def half_rows(core, rows=64):
    return pl.ds(aligned(core * rows, rows), rows)


def shard_greet():
    x, y, z, core = place()
    return [device_at(x, (y + d) % 4, z, core) for d in (1, 2, 3)] + [
        device_at(3 - x, (y + d) % 4, z, core) for d in range(4)
    ]


def greet_all(others):
    barrier = pltpu.get_barrier_semaphore()

    @pl.loop(1, NB)
    def _(shift):
        pl.semaphore_signal(barrier, inc=1, device_id=swap_partner(shift)[1], device_id_type=MESH)

    for other in others:
        pl.semaphore_signal(barrier, inc=1, device_id=other, device_id_type=MESH)
    pl.semaphore_wait(barrier, NB - 1 + len(others))


FRONT_COPIES = 160


def front_kernel(
    tokens, segments, flags, vectors, b_up, w_out, w_up, w_down, w_qkv,
    x_ref, meta_all, heads_all, smalls_all, out_all, up_all, down_all, qkv_all,
    tok_buf, out_buf, up_buf, down_buf, qkv_buf, meta, heads, smalls,
    send, recv, local, meta_send, meta_recv, meta_local,
):
    x, y, z, core = place()
    hi, lo = x // 2, x % 2
    mine, across = y * 2 + hi, y * 2 + 1 - hi
    wrap, pair, other_core = device_at(3 - x, y, z, core), device_at(hi * 2 + 1 - lo, y, z, core), sibling()
    shards, wholes = (up_buf.at[core], down_buf), (up_all, down_all)
    rows_out = half_rows(core)
    loads = [pltpu.make_async_copy(tokens, tok_buf, local.at[0])]
    for j in range(8):
        piece = w_up.at[:, pl.ds(aligned(j * 512 + core * 256, 256), 256)]
        loads.append(pltpu.make_async_copy(piece, up_buf.at[core, :, pl.ds(j * 256, 256)], local.at[1 + j]))
    loads.append(pltpu.make_async_copy(w_out, out_buf, local.at[9]))
    loads.append(pltpu.make_async_copy(w_down.at[half_rows(core, 256)], down_buf, local.at[10]))
    loads.append(pltpu.make_async_copy(w_qkv, qkv_buf, local.at[11]))
    start_all(loads)
    meta[...] = jnp.zeros_like(meta)
    for s in range(2):
        meta[s, 0:1, :] = segments[s : s + 1, :]
        meta[s, 1:2, :] = flags[s : s + 1, :]
    smalls[...] = jnp.zeros_like(smalls)
    smalls[0:8, :] = vectors[...]
    smalls[8:12, :] = b_up[...]
    greet_all(shard_greet())
    loads[0].wait()
    net = Transfers(send, recv)
    first, second = pl.ds(0, 64), pl.ds(64, 64)

    def block(at, low, w, rows=slice(None)):
        return x_ref.at[at, low, core, w, rows]

    swap = net.copy(tok_buf.at[1 - hi], block(z, lo, hi), wrap)
    swap.start()
    own = tok_buf.at[hi]
    own_z = [net.copy(own, block(z, lo, hi), along("z", d)) for d in (1, 3, 2)]
    own_pair = [net.copy(own.at[rows], block(z, lo, hi, rows), pair) for rows in (first, second)]
    start_all([own_pair[0]] + own_z)
    wait_all(loads[1:])
    for p in range(3):
        for k, pair_at in ((0, z * 2 + lo), (1, z * 2 + 1 - lo)):
            heads[k, :, 128 * p : 128 * (p + 1)] = qkv_buf[:, pl.ds(aligned(p * D + pair_at * 128, 128), 128)]
    keep = [
        pltpu.make_async_copy(own, block(z, lo, hi), local.at[0]),
        pltpu.make_async_copy(heads.at[0], heads_all.at[mine], local.at[1]),
        pltpu.make_async_copy(smalls, smalls_all.at[mine], local.at[2]),
        pltpu.make_async_copy(qkv_buf, qkv_all.at[mine], local.at[3]),
    ]
    keep += [pltpu.make_async_copy(shards[m], wholes[m].at[mine], local.at[4 + m]) for m in range(2)]
    keep.append(pltpu.make_async_copy(out_buf, out_all.at[mine], local.at[6]))
    start_all(keep)

    cross_early, cross_late = [], []
    for m in range(2):
        for unit, columns in ((0, columns_part(m, z, 4)), (3, columns_part(m, 1 - lo, 2))):
            rows = unit_rows(m, unit)
            cross_early.append(net.copy(shards[m].at[rows, columns], wholes[m].at[mine, rows, columns], wrap))
        rows = unit_rows(m, 1, 2)
        cross_late.append(net.copy(shards[m].at[rows], wholes[m].at[mine, rows], wrap))
    cross_early.append(net.copy(out_buf.at[rows_out], out_all.at[mine, rows_out], wrap))
    cross_early.append(net.copy(heads.at[1], heads_all.at[mine], wrap))
    cross_early.append(net.copy(smalls, smalls_all.at[mine], wrap))
    start_all(cross_early + cross_late)

    def along_y(shard, source, out_source, heads_source, smalls_source):
        copies = []
        for d in (1, 3, 2):
            there = along("y", d)
            for m in range(2):
                for unit, columns in (
                    (0, columns_part(m, z, 4)),
                    (3, columns_part(m, lo, 2)),
                    (1, slice(None)),
                ):
                    rows = unit_rows(m, unit)
                    copies.append(net.copy(source(m).at[rows, columns], wholes[m].at[shard, rows, columns], there))
            copies.append(net.copy(out_source.at[rows_out], out_all.at[shard, rows_out], there))
            copies.append(net.copy(heads_source, heads_all.at[shard], there))
            copies.append(net.copy(smalls_source, smalls_all.at[shard], there))
        return copies

    meta_start, meta_wait = swap_copies(
        lambda b: meta.at[b % 2], lambda b: meta_all.at[b], (meta_send, meta_recv, meta_local)
    )
    meta_start()
    own_y = along_y(mine, lambda m: shards[m], out_buf, heads.at[0], smalls)
    start_all(own_y)

    swap.wait_recv()
    came = block(z, 1 - lo, 1 - hi)
    came_pair = [
        net.copy(block(z, 1 - lo, 1 - hi, rows), block(z, 1 - lo, 1 - hi, rows), pair) for rows in (first, second)
    ]
    came_z = [net.copy(came, came, along("z", d)) for d in (1, 3, 2)]
    start_all([came_pair[0]] + came_z)
    start_all([own_pair[1], came_pair[1]])

    for copy in cross_early + cross_late:
        copy.wait_recv()
    across_y = along_y(
        across, lambda m: wholes[m].at[across], out_all.at[across], heads_all.at[across], smalls_all.at[across]
    )
    start_all(across_y)

    half_z = []
    for got, low, w in ((own_pair[0], 1 - lo, hi), (came_pair[0], lo, 1 - hi)):
        got.wait_recv()
        piece = block(z, low, w, first)
        half_z += [net.copy(piece, piece, along("z", d)) for d in (1, 3, 2)]
    start_all(half_z)
    pair_late = []
    for i, d in enumerate((1, 3, 2)):
        at = (z + 4 - d) % 4
        for got, low, w in ((own_z[i], lo, hi), (came_z[i], 1 - lo, 1 - hi)):
            got.wait_recv()
            piece = block(at, low, w, second)
            late = net.copy(piece, piece, pair)
            late.start()
            pair_late.append(late)
    keep[0].wait()
    share = []
    for low, w in ((lo, hi), (1 - lo, 1 - hi)):
        piece = x_ref.at[:, low, core, w]
        share.append(net.copy(piece, piece, other_core))
    start_all(share)
    for copy in half_z + [own_pair[1], came_pair[1]] + pair_late:
        copy.wait_recv()
    rest = []
    for low, w in ((1 - lo, hi), (lo, 1 - hi)):
        piece = x_ref.at[:, low, core, w]
        rest.append(net.copy(piece, piece, other_core))
    start_all(rest)
    wait_all(keep[1:])
    meta_wait()
    wait_all(own_y + across_y + share + rest)
    for copy in [swap] + own_pair + own_z + came_pair + came_z + half_z + pair_late + cross_early + cross_late:
        copy.wait_send()


def front(tokens, segments, flags, vectors, b_up, w_out, w_up, w_down, w_qkv):
    shape = jax.ShapeDtypeStruct
    in_vmem = pl.BlockSpec(memory_space=pltpu.VMEM)
    return pl.pallas_call(
        front_kernel,
        in_specs=[ANY] + [in_vmem] * 4 + [ANY] * 4,
        out_specs=[ANY] * 8,
        out_shape=[
            shape((4, 2, 2, 2, TB, D), BF),
            shape((NB, 8, TB), jnp.int32),
            shape((8, 128, 384), BF),
            shape((8, 16, 128), F32),
            shape((8, 128, D), BF),
            shape((8, 128, 2048), BF),
            shape((8, 256, D), BF),
            shape((8, 128, 3 * D), BF),
        ],
        scratch_shapes=[
            pltpu.VMEM((2, TB, D), BF),
            pltpu.VMEM((128, D), BF),
            pltpu.VMEM((2, 128, 2048), BF),
            pltpu.VMEM((256, D), BF),
            pltpu.VMEM((128, 3 * D), BF),
            pltpu.VMEM((2, 8, TB), jnp.int32),
            pltpu.VMEM((2, 128, 384), BF),
            pltpu.VMEM((16, 128), F32),
            pltpu.SemaphoreType.DMA((FRONT_COPIES,)),
            pltpu.SemaphoreType.DMA((FRONT_COPIES,)),
            pltpu.SemaphoreType.DMA((12,)),
            *swap_sems(),
        ],
        name="front_gather",
        compiler_params=pltpu.CompilerParams(
            collective_id=1, has_side_effects=True, vmem_limit_bytes=VMEM_CAP
        ),
    )(tokens, segments, flags, vectors, b_up, w_out, w_up, w_down, w_qkv)


def weights_second(up_all, down_all, out_all, qkv_all, net):
    x, y, z, core = place()
    hi, lo = x // 2, x % 2
    pair, wrap = device_at(hi * 2 + 1 - lo, y, z, core), device_at(3 - x, y, z, core)
    wholes = (up_all, down_all)
    copies = []
    for m in range(2):
        piece = wholes[m].at[:, unit_rows(m, 3), columns_part(m, lo, 2)]
        copies.append(net.copy(piece, piece, pair))
        for d in (1, 3, 2):
            for w in range(2):
                piece = wholes[m].at[y * 2 + w, unit_rows(m, 2)]
                copies.append(net.copy(piece, piece, along("y", d)))
            piece = wholes[m].at[:, unit_rows(m, 0), columns_part(m, z, 4)]
            copies.append(net.copy(piece, piece, along("z", d)))
    piece = out_all.at[:, half_rows(core)]
    copies.append(net.copy(piece, piece, sibling()))
    piece = qkv_all.at[y * 2 + hi, half_rows(core)]
    copies.append(net.copy(piece, piece, wrap))
    return copies


def attend_send_kernel(key_rows, *refs):
    inputs, outputs, wholes, sems = refs[:3], refs[7:10], refs[10:14], refs[14:]
    step = pl.program_id(0)

    def copies():
        return weights_second(*wholes, Transfers(*sems))

    @pl.when(step == 0)
    def _():
        greet(ring_partners())
        start_all(copies())

    attend_kernel(key_rows, *inputs, *outputs)

    @pl.when(step == pl.num_programs(0) - 1)
    def _():
        wait_all(copies())


def attend_send(qat, ka, vat, weights, width=1024, key_rows=512):
    shape = jax.ShapeDtypeStruct
    return pl.pallas_call(
        functools.partial(attend_send_kernel, key_rows),
        grid=(L // width,),
        in_specs=[
            pl.BlockSpec((128, width), lambda i: (0, i)),
            pl.BlockSpec((L, 128), lambda i: (0, 0)),
            pl.BlockSpec((80, L), lambda i: (0, 0)),
        ]
        + [ANY] * 4,
        out_specs=[
            pl.BlockSpec((width // TB, HD, TB), lambda i: (i, 0, 0)),
            pl.BlockSpec((HD, width), lambda i: (0, i)),
            pl.BlockSpec((1, width), lambda i: (0, i)),
        ]
        + [ANY] * 4,
        out_shape=[shape((NB, HD, TB), BF), shape((HD, L), F32), shape((1, L), F32)]
        + [shape(w.shape, w.dtype) for w in weights],
        input_output_aliases={3: 3, 4: 4, 5: 5, 6: 6},
        scratch_shapes=[pltpu.SemaphoreType.DMA((24,)), pltpu.SemaphoreType.DMA((24,))],
        name="attend",
        compiler_params=pltpu.CompilerParams(
            collective_id=2, has_side_effects=True, vmem_limit_bytes=VMEM_CAP
        ),
    )(qat, ka, vat, *weights)


def qkv_along_y(qkv_all, net):
    _, y, _, core = place()
    copies = []
    for d in (1, 3, 2):
        for w in range(2):
            piece = qkv_all.at[y * 2 + w, half_rows(core)]
            copies.append(net.copy(piece, piece, along("y", d)))
    return copies


def turned(first, second):
    return dot(first, second, ((0,), (0,)))


def gelu_both(u):
    rate = 0.7978845608028654
    square = u * u
    curve = jnp.tanh(rate * (u + 0.044715 * (square * u)))
    half = 0.5 * (1.0 + curve)
    slope = half + 0.5 * u * (1.0 - curve * curve) * (rate * (1.0 + 0.134145 * square))
    return u * half, slope


def fold(values):
    return jnp.sum(values.reshape(values.shape[0] // 8, 8, values.shape[1]), axis=0)


ROWS = 256
CHUNK = 32
SMALLS = 16


def middle_kernel(
    blocks, meta, tokens, teacher, flags, smalls, out_all, up_all, down_all, a0,
    states, resid_out, do, g_ref, sums_out, count_out, qkv_all,
    context, context_s, w_out, w_up, w_down, h, act, slope, send_one, come_one, send_two, come_two,
    gb, gu, ga, ga_s, normed, hidden, rate, work, resid, gct, stage, count, counts, valid,
    send, recv, local, go_send, go_recv, go_local, back_send, back_recv, back_local,
):
    x, y, z, core = place()
    mine = y * 2 + x // 2
    twin = sibling()
    loads = [
        pltpu.make_async_copy(out_all, w_out, local.at[0]),
        pltpu.make_async_copy(up_all, w_up, local.at[1]),
        pltpu.make_async_copy(down_all, w_down, local.at[2]),
    ]
    start_all(loads)
    greet_all(shard_greet())
    net = Transfers(send, recv)
    go_start, go_wait = swap_copies(
        lambda b: blocks.at[b], lambda b: head_tile(context, b), (go_send, go_recv, go_local)
    )
    go_start()
    valid_here = jnp.sum(meta[:, 1, :].astype(F32), axis=0, keepdims=True)
    count[...] = jnp.broadcast_to(jnp.sum(valid_here, axis=1, keepdims=True), (8, 128))
    ahead = [net.copy(count, counts.at[mine], target) for target in shard_greet()]
    start_all(ahead)
    own_count = pltpu.make_async_copy(count, counts.at[mine], local.at[3])
    own_count.start()
    later = qkv_along_y(qkv_all, net)
    start_all(later)
    for s in range(2):
        column = jnp.broadcast_to(flags[s : s + 1, :].astype(F32), (128, 128)).T
        valid[128 * s : 128 * (s + 1), :] = column

    def vector(row):
        return jnp.concatenate([smalls[i, row : row + 1, :] for i in range(8)], axis=1)

    out_bias, gain_one, offset_one, down_bias, gain_two, offset_two = [vector(row) for row in range(2, 8)]
    zeros = jnp.zeros((8, D), F32)
    go_wait()
    give_context = net.copy(context, context_s, twin)
    give_context.start()
    wait_all(loads)
    work[...] = turned(context[...], w_out[...].reshape(D, D))

    @pl.loop(0, ROWS // CHUNK)
    def _(i):
        rows = pl.ds(aligned(i * CHUNK, CHUNK), CHUNK)
        total = tokens[rows, :].astype(F32) + work[rows, :] + out_bias
        centre = total - jnp.mean(total, axis=1, keepdims=True)
        scale = lax.rsqrt(jnp.mean(centre * centre, axis=1, keepdims=True) + EPS)
        unit = centre * scale
        normed[rows, :] = unit
        rate[rows, :] = jnp.broadcast_to(scale, (CHUNK, 128))
        full = unit * gain_one + offset_one
        hidden[rows, :] = full
        h[0, rows, :] = full.astype(BF)

    give_hidden = net.copy(h.at[0], h.at[1], twin)
    give_hidden.start()
    for slot in range(2):
        if slot == 1:
            give_hidden.wait()
        for k in range(8):
            columns = slice(256 * k, 256 * (k + 1))
            bias = jnp.concatenate([smalls[k, pl.ds(8 + 2 * core + e, 1), :] for e in range(2)], axis=1)
            u = dot(h[slot], w_up[:, :, columns].reshape(D, 256)) + bias
            value, incline = gelu_both(u)
            act[slot, :, columns] = value.astype(BF)
            slope[slot, :, columns] = incline
    send_one[...] = dot(act[1], w_down[...].reshape(2048, D))
    give_one = net.copy(send_one, come_one, twin)
    give_one.start()
    work[...] = dot(act[0], w_down[...].reshape(2048, D))
    give_one.wait()
    wait_all(ahead)
    own_count.wait()
    total_count = jnp.sum(counts[...], axis=0)
    count_out[...] = total_count
    factor = (128 * ROWS) / total_count[:1, :1]

    def loss_rows(i, carried):
        rows = pl.ds(aligned(i * CHUNK, CHUNK), CHUNK)
        total = hidden[rows, :] + (work[rows, :] + come_one[rows, :] + down_bias)
        centre = total - jnp.mean(total, axis=1, keepdims=True)
        scale = lax.rsqrt(jnp.mean(centre * centre, axis=1, keepdims=True) + EPS)
        unit = centre * scale
        final = unit * gain_two + offset_two
        states[rows, :] = final.astype(BF)
        differ = final - teacher[rows, :].astype(F32)
        held = valid[rows, :1] * differ
        grad = factor * held
        weighted = grad * gain_two
        back = weighted - jnp.mean(weighted, axis=1, keepdims=True)
        back = scale * (back - unit * jnp.mean(weighted * unit, axis=1, keepdims=True))
        resid[rows, :] = back
        low = back.astype(BF)
        gb[0, rows, :] = low
        return (
            carried[0] + fold(grad * unit),
            carried[1] + fold(grad),
            carried[2] + fold(low.astype(F32)),
            carried[3] + fold(held * differ),
        )

    gain_two_sum, offset_two_sum, down_sum, error = lax.fori_loop(
        0, ROWS // CHUNK, loss_rows, (zeros, zeros, zeros, zeros)
    )
    give_branch = net.copy(gb.at[0], gb.at[1], twin)
    give_branch.start()
    up_sums = []
    for slot in range(2):
        if slot == 1:
            give_branch.wait()
        for k in range(8):
            columns = slice(256 * k, 256 * (k + 1))
            pulled = dot(gb[slot], w_down[k], ((1,), (1,))) * slope[slot, :, columns]
            low = pulled.astype(BF)
            gu[slot, :, columns] = low
            up_sums.append(fold(low.astype(F32)))
    for i in range(8):
        send_two[:, 128 * i : 128 * (i + 1)] = dot(gu[1], w_up[i], ((1,), (1,)))
    give_two = net.copy(send_two, come_two, twin)
    give_two.start()
    for i in range(8):
        work[:, 128 * i : 128 * (i + 1)] = dot(gu[0], w_up[i], ((1,), (1,)))
    give_two.wait()

    def first_norm_rows(i, carried):
        rows = pl.ds(aligned(i * CHUNK, CHUNK), CHUNK)
        grad = resid[rows, :] + (work[rows, :] + come_two[rows, :])
        unit = normed[rows, :]
        weighted = grad * gain_one
        back = weighted - jnp.mean(weighted, axis=1, keepdims=True)
        back = rate[rows, :1] * (back - unit * jnp.mean(weighted * unit, axis=1, keepdims=True))
        resid_out[rows, :] = back
        low = back.astype(BF)
        ga[rows, :] = low
        return (carried[0] + fold(grad * unit), carried[1] + fold(grad), carried[2] + fold(low.astype(F32)))

    gain_one_sum, offset_one_sum, out_sum = lax.fori_loop(0, ROWS // CHUNK, first_norm_rows, (zeros, zeros, zeros))
    give_attended = net.copy(ga.at[:, pl.ds(aligned((1 - core) * 512, 512), 512)], ga_s, twin)
    give_attended.start()
    gct[...] = dot(w_out[...].reshape(D, D), ga[...], ((1,), (1,))).astype(BF)
    back_start, back_wait = swap_copies(
        lambda b: head_tile(gct, b), lambda b: do.at[b], (back_send, back_recv, back_local)
    )
    back_start()

    error = jnp.broadcast_to(jnp.sum(jnp.sum(error, axis=0, keepdims=True), axis=1, keepdims=True), (1, 128))
    lines = [out_sum, gain_one_sum, offset_one_sum, down_sum, gain_two_sum, offset_two_sum]
    lines = [jnp.sum(line, axis=0, keepdims=True) for line in lines]
    for i in range(8):
        columns = slice(128 * i, 128 * (i + 1))
        sums_out[i] = jnp.zeros((SMALLS, 128), F32)
        for row, line in enumerate(lines):
            sums_out[i, row : row + 1, :] = line[:, columns]
        both = jnp.sum(up_sums[i] + up_sums[8 + i], axis=0, keepdims=True)
        for e in range(2):
            sums_out[i, pl.ds(6 + 2 * core + e, 1), :] = both[:, 128 * e : 128 * (e + 1)]
        sums_out[i, 10:11, :] = error

    give_context.wait()
    give_attended.wait()

    def stored(i):
        return pltpu.make_async_copy(stage.at[i % 2], g_ref.at[i // 2, i % 2], local.at[4 + i % 2])

    for i in range(8):
        if i >= 2:
            stored(i - 2).wait()
        tall = slice(128 * i, 128 * (i + 1))
        wide = slice(256 * i, 256 * (i + 1))
        up = turned(h[0, :, tall], gu[0]) + turned(h[1, :, tall], gu[1])
        for k in range(4):
            stage[i % 2, 128 * k : 128 * (k + 1), :] = up[:, 512 * k : 512 * (k + 1)].astype(BF)
        down = turned(act[0, :, wide], gb[0]) + turned(act[1, :, wide], gb[1])
        for k in range(2):
            stage[i % 2, 512 + 256 * k : 768 + 256 * k, :] = down[:, 512 * k : 512 * (k + 1)].astype(BF)
        own_half = ga[:, pl.ds(aligned(core * 512, 512), 512)]
        out = dot(context[tall, :], own_half) + dot(context_s[tall, :], ga_s[...])
        stage[i % 2, 1024:, :] = out.astype(BF)
        stored(i).start()
    stored(6).wait()
    stored(7).wait()
    back_wait()
    wait_all(later)


def middle(blocks, meta, tokens, teacher, flags, smalls, out_all, up_all, down_all, qkv_all):
    shape = jax.ShapeDtypeStruct
    in_vmem = pl.BlockSpec(memory_space=pltpu.VMEM)
    dma = pltpu.SemaphoreType.DMA
    wide = pltpu.VMEM((ROWS, D), F32)
    return pl.pallas_call(
        middle_kernel,
        in_specs=[ANY] + [in_vmem] * 5 + [ANY] * 4,
        out_specs=[in_vmem, in_vmem, ANY, ANY, in_vmem, in_vmem, ANY],
        out_shape=[
            shape((ROWS, D), BF),
            shape((ROWS, D), F32),
            shape((NB, HD, TB), BF),
            shape((4, 2, 1152, 512), BF),
            shape((8, SMALLS, 128), F32),
            shape((8, 128), F32),
            shape(qkv_all.shape, BF),
        ],
        input_output_aliases={9: 6},
        scratch_shapes=[
            pltpu.VMEM((D, ROWS), BF),
            pltpu.VMEM((D, ROWS), BF),
            pltpu.VMEM((8, 128, D), BF),
            pltpu.VMEM((8, 128, 2048), BF),
            pltpu.VMEM((8, 256, D), BF),
            pltpu.VMEM((2, ROWS, D), BF),
            pltpu.VMEM((2, ROWS, 2048), BF),
            pltpu.VMEM((2, ROWS, 2048), F32),
            wide,
            wide,
            wide,
            wide,
            pltpu.VMEM((2, ROWS, D), BF),
            pltpu.VMEM((2, ROWS, 2048), BF),
            pltpu.VMEM((ROWS, D), BF),
            pltpu.VMEM((ROWS, 512), BF),
            wide,
            wide,
            pltpu.VMEM((ROWS, 128), F32),
            wide,
            wide,
            pltpu.VMEM((D, ROWS), BF),
            pltpu.VMEM((2, 1152, 512), BF),
            pltpu.VMEM((8, 128), F32),
            pltpu.VMEM((8, 8, 128), F32),
            pltpu.VMEM((ROWS, 128), F32),
            dma((24,)),
            dma((24,)),
            dma((8,)),
            *swap_sems(),
            *swap_sems(),
        ],
        name="middle",
        compiler_params=pltpu.CompilerParams(
            collective_id=3, has_side_effects=True, vmem_limit_bytes=VMEM_CAP
        ),
    )(blocks, meta, tokens, teacher, flags, smalls, out_all, up_all, down_all, qkv_all)


def attend_back_send_kernel(key_rows, *refs):
    inputs, g_ref, dqkv_ref, f_ref = refs[:8], refs[8], refs[9], refs[10]
    dk_ref, dv_ref = refs[11:13]
    net = (g_ref,) + refs[13:]
    step = pl.program_id(0)
    steps = pl.num_programs(0)

    @pl.when(step == 0)
    def _():
        greet(ring_partners()[:9])
        reduce_start(net)

    attend_back_kernel(key_rows, *inputs, dqkv_ref, dk_ref, dv_ref)

    @pl.when(step == steps - 2)
    def _():
        reduce_step(0, net)

    @pl.when(step == steps - 1)
    def _():
        reduce_step(1, net)
        reduce_step(2, net)
        f_ref[...] = net[7][:, 0]


def attend_back_send(qat, ka, va, kt, q8, do, wide, lse, g, width=512, key_rows=512):
    def whole(shape):
        return pl.BlockSpec(shape, lambda i: (0,) * len(shape))

    return pl.pallas_call(
        functools.partial(attend_back_send_kernel, key_rows),
        grid=(L // width,),
        in_specs=[
            pl.BlockSpec((128, width), lambda i: (0, i)),
            whole((L, 128)),
            whole((L, 128)),
            whole((HD, L)),
            pl.BlockSpec((width, HD), lambda i: (i, 0)),
            pl.BlockSpec((width // TB, HD, TB), lambda i: (i, 0, 0)),
            pl.BlockSpec((HD, width), lambda i: (0, i)),
            pl.BlockSpec((1, width), lambda i: (0, i)),
            ANY,
        ],
        out_specs=[whole((NB, 3 * HD, TB)), whole((3, 48, 512))],
        out_shape=[jax.ShapeDtypeStruct((NB, 3 * HD, TB), BF), jax.ShapeDtypeStruct((3, 48, 512), BF)],
        scratch_shapes=[pltpu.VMEM((L, HD), F32), pltpu.VMEM((L, HD), F32)] + reduce_scratch(),
        name="attend_back",
        compiler_params=pltpu.CompilerParams(
            collective_id=5, has_side_effects=True, vmem_limit_bytes=VMEM_CAP
        ),
    )(qat, ka, va, kt, q8, do, wide, lse, g)


def last_kernel(
    dqkv, x_seq, pieces, smalls, a0,
    projected, heads_out, shard_out, smalls_out, qkv_all,
    d_ref, x_buf, mine_ref, parts_ref, sum_ref, small_buf, small_sum, small_all, f_ref, heads_buf,
    spread_send, spread_recv, local, send, recv, swap_send, swap_recv, swap_local,
):
    x, y, z, core = place()
    shard_at = y * 2 + x // 2
    seq = lax.axis_index("seq")

    def shard_device(d):
        other = (shard_at + d) % 8
        return other, (other // 2, seq, other % 2)

    greet_all([shard_device(d)[1] for d in range(1, 8)])
    net = Transfers(send, recv)
    start, wait = swap_copies(
        lambda b: dqkv.at[b], lambda b: head_tile3(projected, b), (swap_send, swap_recv, swap_local)
    )
    start()
    load = [
        pltpu.make_async_copy(dqkv, d_ref, local.at[3]),
        pltpu.make_async_copy(pieces, f_ref, local.at[4]),
    ]
    start_all(load)
    small_out = [net.copy(smalls.at[shard_device(d)[0]], small_buf.at[shard_at], shard_device(d)[1]) for d in range(1, 8)]
    small_own = pltpu.make_async_copy(smalls.at[shard_at], small_buf.at[shard_at], local.at[5])
    start_all(small_out + [small_own])
    rows = pl.ds(aligned(core * 64, 64), 64)
    weights = net.copy(qkv_all.at[:, rows], qkv_all.at[:, rows], sibling())
    weights.start()

    def chunk(j):
        return pltpu.make_async_copy(x_seq.at[pl.ds(j * 4, 4)], x_buf.at[j % 2], local.at[6 + j % 2])

    chunk(0).start()
    load[1].wait()
    spread_begin, spread_middle, spread_end = spread_steps((f_ref, local, spread_send, spread_recv), shard_out)
    spread_begin()
    load[0].wait()
    total = jnp.zeros((3 * HD, D), F32)
    sums = jnp.zeros((8, 3 * HD), F32)
    for j in range(8):
        chunk(j).wait()
        if j < 7:
            chunk(j + 1).start()
        left = jnp.concatenate([d_ref[4 * j + k].reshape(3 * HD, TB) for k in range(4)], axis=1)
        total = total + dot(left, x_buf[j % 2].reshape(4 * TB, D))
        sums = sums + dot(jnp.ones((8, 4 * TB), BF), left, ((1,), (1,)))
    gap = jnp.zeros((1, 128 - HD), F32)
    tail = jnp.concatenate(
        [
            jnp.concatenate([sums[:1, :HD], gap], axis=1),
            jnp.concatenate([sums[:1, 2 * HD :], gap], axis=1),
            jnp.zeros((14, 128), F32),
        ],
        axis=0,
    ).astype(BF)
    for i in range(8):
        mine_ref[i, : 3 * HD, :] = total[:, 128 * i : 128 * (i + 1)].astype(BF)
        mine_ref[i, 3 * HD :, :] = tail
    part_out = [net.copy(mine_ref.at[shard_device(d)[0]], parts_ref.at[d], shard_device(d)[1]) for d in range(1, 8)]
    start_all(part_out)
    wait_all(small_out + [small_own])
    small_sum[...] = jnp.sum(small_buf[...], axis=0)
    spread_middle()
    wait_all(part_out)
    added = mine_ref[shard_at].astype(F32)
    for d in range(1, 8):
        added = added + parts_ref[d].astype(F32)
    sum_ref[...] = added.astype(BF)
    head_out = []
    for d in range(1, 16):
        other = (seq + d) % 16
        target = (y, other, x // 2)
        head_out.append(net.copy(sum_ref, heads_buf.at[seq], target))
        head_out.append(net.copy(small_sum, small_all.at[seq], target))
    head_own = [
        pltpu.make_async_copy(sum_ref, heads_buf.at[seq], local.at[3]),
        pltpu.make_async_copy(small_sum, small_all.at[seq], local.at[4]),
    ]
    start_all(head_out + head_own)
    wait()
    spread_end()
    weights.wait()
    wait_all(head_out + head_own)
    heads_out[...] = heads_buf[...]
    smalls_out[...] = jnp.sum(small_all[...], axis=0)


def spread_steps(refs, o_ref):
    mine_ref, local, send, recv = refs
    x, y, z, core = place()
    low = x % 2
    pair = device_at(x // 2 * 2 + 1 - low, y, z, core)
    first, own, second, third = [], [], [], []
    for part in range(3):
        mine = mine_ref.at[part]
        own.append(pltpu.make_async_copy(mine, shard_rows(o_ref, part, low, z, core), local.at[part]))
        first.append(remote(mine, shard_rows(o_ref, part, low, z, core), send.at[part, 0], recv.at[part, 0], pair))
        for shift in (1, 2, 3):
            spot = shard_rows(o_ref, part, low, z, core)
            second.append(remote(mine, spot, send.at[part, shift], recv.at[part, shift], along("z", shift)))
            spot = shard_rows(o_ref, part, 1 - low, z, core)
            third.append(remote(spot, spot, send.at[part, 3 + shift], recv.at[part, 3 + shift], along("z", shift)))

    def begin():
        start_all(own + first + second)

    def middle():
        wait_all(first)
        start_all(third)

    def end():
        wait_all(own + second + third)
        rows = o_ref.at[core]
        across = remote(rows, rows, send.at[0, 7], recv.at[0, 7], sibling())
        across.start()
        across.wait()

    return begin, middle, end


def last_swap(dqkv, x_seq, pieces, smalls, qkv_all):
    shape = jax.ShapeDtypeStruct
    in_vmem = pl.BlockSpec(memory_space=pltpu.VMEM)
    dma = pltpu.SemaphoreType.DMA
    return pl.pallas_call(
        last_kernel,
        in_specs=[ANY] * 5,
        out_specs=[ANY, in_vmem, ANY, in_vmem, ANY],
        out_shape=[
            shape((3, D, 2 * TB), BF),
            shape((H, 208, 128), BF),
            shape((2, 1152, 512), BF),
            shape((16, 128), F32),
            shape(qkv_all.shape, BF),
        ],
        input_output_aliases={4: 4},
        scratch_shapes=[
            pltpu.VMEM((NB, 3, HD, TB), BF),
            pltpu.VMEM((2, 4, TB, D), BF),
            pltpu.VMEM((8, 208, 128), BF),
            pltpu.VMEM((8, 208, 128), BF),
            pltpu.VMEM((208, 128), BF),
            pltpu.VMEM((8, 16, 128), F32),
            pltpu.VMEM((16, 128), F32),
            pltpu.VMEM((16, 16, 128), F32),
            pltpu.VMEM((3, 48, 512), BF),
            pltpu.VMEM((H, 208, 128), BF),
            dma((3, 8)),
            dma((3, 8)),
            dma((8,)),
            dma((48,)),
            dma((48,)),
            *swap_sems(),
        ],
        name="last_swap",
        compiler_params=pltpu.CompilerParams(
            collective_id=6, has_side_effects=True, vmem_limit_bytes=VMEM_CAP
        ),
    )(dqkv, x_seq, pieces, smalls, qkv_all)


def finish_kernel(
    projected, qkv_ref, resid_ref, heads_ref, shard_ref, tokens_ref, grad_qkv, grad_out, grad_up, grad_down
):
    step = pl.program_id(0)
    tokens_ref[...] = resid_ref[...] + dot(projected[...], qkv_ref[...], ((0,), (1,)))
    for c in range(2):
        columns = slice(512 * c, 512 * (c + 1))
        for j in range(2):
            piece = shard_ref[c, pl.ds(aligned(step * 128, 128), 128), 256 * j : 256 * (j + 1)]
            grad_up[:, 512 * j + 256 * c : 512 * j + 256 * (c + 1)] = piece.astype(F32)
        rows = pl.ds(aligned(512 + 256 * c + (step % 2) * 128, 128), 128)
        grad_down[:, columns] = shard_ref[step // 2, rows, :].astype(F32)
        grad_out[:, columns] = shard_ref[c, pl.ds(aligned(1024 + step * 32, 32), 32), :].astype(F32)

    @pl.when(step == 0)
    def _():
        for p in range(3):
            for pair in range(8):
                both = [heads_ref[2 * pair + k, p * HD : (p + 1) * HD, :].astype(F32) for k in range(2)]
                at = p * D + pair * 128
                grad_qkv[:, at : at + 128] = jnp.concatenate(both, axis=0).T


def finish(projected, qkv, resid, heads, shard):
    shape = jax.ShapeDtypeStruct

    def whole(dims):
        return pl.BlockSpec(dims, lambda i: (0,) * len(dims))

    return pl.pallas_call(
        finish_kernel,
        grid=(4,),
        in_specs=[
            whole((3 * D, 2 * TB)),
            pl.BlockSpec((256, 3 * D), lambda i: (i, 0)),
            pl.BlockSpec((2 * TB, 256), lambda i: (0, i)),
            whole((H, 208, 128)),
            whole((2, 1152, 512)),
        ],
        out_specs=[
            pl.BlockSpec((2 * TB, 256), lambda i: (0, i)),
            whole((128, 3 * D)),
            pl.BlockSpec((32, D), lambda i: (i, 0)),
            pl.BlockSpec((128, 1024), lambda i: (0, i)),
            pl.BlockSpec((128, D), lambda i: (i, 0)),
        ],
        out_shape=[
            shape((2 * TB, D), F32),
            shape((128, 3 * D), F32),
            shape((128, D), F32),
            shape((128, FF), F32),
            shape((512, D), F32),
        ],
        name="finish",
        compiler_params=pltpu.CompilerParams(vmem_limit_bytes=VMEM_CAP),
    )(projected, qkv, resid, heads, shard)


def on_device(
    tokens,
    segments,
    valid_flags,
    teacher,
    w_qkv,
    b_query,
    b_value,
    w_out,
    b_out,
    ln1_gain,
    ln1_bias,
    w_up,
    b_up,
    w_down,
    b_down,
    ln2_gain,
    ln2_bias,
):
    seq_local, row_local, _ = tokens.shape
    token_rows = seq_local * row_local
    shard_at = lax.axis_index("dp") * 2 + lax.axis_index("wshard")

    vectors = jnp.stack([b_query, b_value, b_out, ln1_gain, ln1_bias, b_down, ln2_gain, ln2_bias]).astype(F32)
    x_seq, meta_all, heads_all, smalls_all, out_all, up_all, down_all, qkv_all = front(
        tokens, segments, valid_flags, vectors, b_up.reshape(4, 128).astype(F32), w_out, w_up, w_down, w_qkv
    )
    x_seq = x_seq.reshape(NB, TB, D)
    qat, ka, vat, va, kt, q8 = project(x_seq.reshape(L, D), heads_all.reshape(D, 384), smalls_all, meta_all)
    blocks, wide, lse, up_all, down_all, out_all, qkv_all = attend_send(
        qat, ka, vat, (up_all, down_all, out_all, qkv_all)
    )
    states, grad_resid_one, do, g, small_sums, count, qkv_all = middle(
        blocks,
        meta_all,
        tokens.reshape(token_rows, D),
        teacher.reshape(token_rows, D),
        valid_flags,
        smalls_all,
        out_all,
        up_all,
        down_all,
        qkv_all,
    )
    dqkv, pieces = attend_back_send(qat, ka, va, kt, q8, do, wide, lse, g)
    projected, heads_out, shard_out, small_out, qkv_all = last_swap(
        dqkv.reshape(NB, 3, HD, TB), x_seq, pieces, small_sums, qkv_all
    )
    grad_tokens, grad_qkv, grad_out, grad_up, grad_down = finish(
        projected.reshape(3 * D, token_rows), qkv_all.reshape(D, 3 * D), grad_resid_one, heads_out, shard_out
    )
    own_heads = lax.dynamic_slice(heads_out, (shard_at * 2, 3 * HD, 0), (2, 2, HD)).astype(F32)
    mean_loss = small_out[10, 0] / (D * count[0, 0])
    return (
        states.reshape(seq_local, row_local, D),
        mean_loss,
        grad_tokens.reshape(seq_local, row_local, D),
        grad_qkv,
        own_heads[:, 0].reshape(128),
        own_heads[:, 1].reshape(128),
        grad_out,
        small_out[0],
        small_out[1],
        small_out[2],
        grad_up,
        small_out[6:10].reshape(512),
        grad_down,
        small_out[3],
        small_out[4],
        small_out[5],
    )


def solution(mesh):
    rows = P("dp", ("seq", "wshard"), None)
    flags = P("dp", ("seq", "wshard"))
    matrix = P(("dp", "wshard"), None)
    vector = P(("dp", "wshard"))
    return jax.shard_map(
        on_device,
        mesh=mesh,
        in_specs=(
            rows,
            flags,
            flags,
            rows,
            matrix,
            vector,
            vector,
            matrix,
            vector,
            vector,
            vector,
            matrix,
            vector,
            matrix,
            vector,
            vector,
            vector,
        ),
        out_specs=(
            rows,
            P(),
            rows,
            matrix,
            vector,
            vector,
            matrix,
            vector,
            vector,
            vector,
            matrix,
            vector,
            matrix,
            vector,
            vector,
            vector,
        ),
        check_vma=False,
    )
```

time: 1610 us -> 314 us (0.20)
  waiting for transfers between devices: 565 us -> 0 us
  blocking collectives: 510 us -> 0 us
  Pallas kernels: 0 us -> 299 us
  matrix products: 229 us -> 0 us
  other arithmetic: 127 us -> 2.53 us
  local copies, waits for them, and re-layouts: 112 us -> 5.62 us
  starting transfers between devices: 38.3 us -> 0 us
  between operations: 20.3 us -> 3.34 us
    reduce_scatter x3 -> x0, waiting for transfers between devices: 309 us -> none  [the longest x1 119 us: on_device(): lax.psum_scatter(grad_up.astype(jnp.bfloat16), ('dp', 'wshard'), scatter_...]
    pallas_call x0 -> x7, Pallas kernels: none -> 299 us  [the longest x1 76.7 us: front(): pl.pallas_call(front_kernel, in_specs=[ANY] + [in_vmem] * 4 + [ANY] * 4,...]
    dot_general x68 -> x0, matrix products: 229 us -> none  [the longest x16 57.1 us: block_scores(): jnp.einsum('qhd,khd->hqk', queries, keys_all, preferred_element_type=jnp....]
    all_gather x10 -> x0, blocking collectives: 221 us -> none  [the longest x1 63.1 us: on_device(): lax.all_gather(segments, ('seq', 'wshard'), axis=1, tiled=True)]
    psum x3 -> x0, blocking collectives: 204 us -> none  [the longest x2 170 us: on_device(): lax.psum((jnp.sum(valid_col * differ * differ), jnp.sum(valid_col)), ('dp...]
    unnamed x13 -> x0, waiting for transfers between devices: 188 us -> none
    convert_element_type x28 -> x3, other arithmetic: 92 us -> 2.53 us  [the longest x1 1.26 us: on_device(): b_up.reshape(4, 128).astype(F32)]
    all_gather x5 -> x0, waiting for transfers between devices: 58.4 us -> none  [the longest x1 58.4 us: on_device(): lax.all_gather(w_qkv, ('dp', 'wshard'), axis=0, tiled=True)]
  transfers between devices with their start and end apart: 13 -> 0, of which waited for: 7 -> 0; matrix products, arithmetic and copies ran while one was open for 6% -> 0% of each run, Pallas kernels for 0% -> 0%
where the time goes in v1:
time: 314 us; the launch traced here: 311 us
  Pallas kernels  299 us (95%)
  local copies, waits for them, and re-layouts  5.62 us (2%)
  between operations  3.34 us (1%)
    pallas_call x1, Pallas kernels, front(): pl.pallas_call(front_kernel, in_specs=[ANY] + [in_vmem] * 4 + [ANY] * 4,...  76.7 us
    pallas_call x1, Pallas kernels, middle(): pl.pallas_call(middle_kernel, in_specs=[ANY] + [in_vmem] * 5 + [ANY] * 4,...  63.2 us
    pallas_call x1, Pallas kernels, attend_back_send(): pl.pallas_call(functools.partial(attend_back_send_kernel, key_rows), grid...  59.3 us
    pallas_call x1, Pallas kernels, last_swap(): pl.pallas_call(last_kernel, in_specs=[ANY] * 5, out_specs=[ANY, in_vmem,...  51.3 us
    pallas_call x1, Pallas kernels, attend_send(): pl.pallas_call(functools.partial(attend_send_kernel, key_rows), grid=(L /...  29.4 us
    pallas_call x1, Pallas kernels, project(): pl.pallas_call(project_kernel, grid=(L // rows,), in_specs=[pl.BlockSpec(...  9.88 us
    pallas_call x1, Pallas kernels, finish(): pl.pallas_call(finish_kernel, grid=(4,), in_specs=[whole((3 * D, 2 * TB))...  9.52 us

profile of v1, /device:TPU:1, one launch (start us, length us, event | category | flops | bytes accessed | tf_op | source)
XLA Modules:
  0.0 310.8 jit_solution(16771730449933563048)
XLA Ops:
  0.6 0.8 stack.35
  1.4 0.6 convert_element_type.11.vectors
  2.0 1.3 bitcast_convert_fusion.b_up
  3.3 76.7 %front_gather.1 = (bf16[4,2,2,2,128,1024]{5,4,3,2,1,0:T(8,128)(2,1)}, s32[32,8,128]{2,1,0:T(8,128)}, bf16[8,128,384]{2,1,0:T(8,128)(2,1)}, f32[8,16,128]{2,1,0:T...) custom-call(bf16[2,128,1024]{2,1,0:T(8,128)(2,1)} %tokens.1, ...), custom_call_target="tpu_custom_call" | custom-call | tf_op jit(solution)/shard_map/front_gather/pallas_call | solution.py:703
  80.0 9.9 %project_head.1 = (bf16[128,4096]{1,0:T(8,128)(2,1)}, bf16[4096,128]{1,0:T(8,128)(2,1)}, bf16[80,4096]{1,0:T(8,128)(2,1)}, bf16[4096,128]{1,0:T(8,128)(2,1)}, bf...) custom-call(bf16[4096,1024]{1,0:T(8,128)(2,1)} %bitcast.37, bf16[1024,384]{1,0:T(8,128)(2,1)} %bitcast.42, ...), custom_call_target="tpu_custom_call" | custom-call | tf_op jit(solution)/shard_map/project_head/pallas_call | solution.py:71
  89.9 29.4 %attend.1 = (bf16[32,64,128]{2,1,0:T(8,128)(2,1)}, f32[64,4096]{1,0:T(8,128)}, f32[1,4096]{1,0:T(1,128)}, bf16[8,128,2048]{2,1,0:T(8,128)(2,1)}, bf16[8,256,1024...) custom-call(bf16[128,4096]{1,0:T(8,128)(2,1)} %get-tuple-element.60., ...), custom_call_target="tpu_custom_call", output_to_operand_aliasing={{3}: (3, {}), {4}: (4, {}), {5}: (5, {}), {6}: (6, {})} | custom-call | tf_op jit(solution)/shard_map/attend/pallas_call | solution.py:781
  119.3 63.2 %middle.1 = (bf16[256,1024]{1,0:T(8,128)(2,1)}, f32[256,1024]{1,0:T(8,128)}, bf16[32,64,128]{2,1,0:T(8,128)(2,1)}, bf16[4,2,1152,512]{3,2,1,0:T(8,128)(2,1)}, f3...) custom-call(bf16[32,64,128]{2,1,0:T(8,128)(2,1)} %get-tuple-element.6, ...), custom_call_target="tpu_custom_call", output_to_operand_aliasing={{6}: (9, {})} | custom-call | tf_op jit(solution)/shard_map/middle/pallas_call | solution.py:1033
  182.5 59.3 %attend_back.1 = (bf16[32,192,128]{2,1,0:T(8,128)(2,1)}, bf16[3,48,512]{2,1,0:T(8,128)(2,1)}) custom-call(bf16[128,4096]{1,0:T(8,128)(2,1)} %get-tuple-element.60.refs_0_, bf16[4096,128]{1,0:T(8,128)(2,1)} %get-tuple-element.61.refs_1_, bf16[4096,128]{1,0:T(8,128)(2,1)} %get-tuple-element.73.refs_2_, bf16[64,4096]{1,0:T(8,128)(2,1)} %get-tuple-element.74.refs_3_, ...), custom_call_target="tpu_custom_call" | custom-call | tf_op jit(solution)/shard_map/attend_back/pallas_call | solution.py:1116
  241.8 51.3 %last_swap.1 = (bf16[3,1024,256]{2,1,0:T(8,128)(2,1)}, bf16[16,208,128]{2,1,0:T(8,128)(2,1)}, bf16[2,1152,512]{2,1,0:T(8,128)(2,1)}, f32[16,128]{1,0:T(8,128)}, bf16[8,128,3072]{2,1,0:T(8,128)(2,1)}) custom-call(bf16[32,3,64,128]{3,2,1,0:T(8,128)(2,1)} %bitcast.40, bf16[32,128,1024]{2,1,0:T(8,128)(2,1)} %bitcast.38, ...), custom_call_target="tpu_custom_call", output_to_operand_aliasing={{4}: (4, {})} | custom-call | tf_op jit(solution)/shard_map/last_swap/pallas_call | solution.py:1267
  293.1 0.0 copy-start.1
  293.1 0.0 copy-start
  293.1 9.5 %finish.1 = (f32[256,1024]{1,0:T(8,128)}, f32[128,3072]{1,0:T(8,128)}, f32[128,1024]{1,0:T(8,128)}, f32[128,4096]{1,0:T(8,128)}, f32[512,1024]{1,0:T(8,128)}) custom-call(bf16[3072,256]{1,0:T(8,128)(2,1)} %bitcast.41, bf16[1024,3072]{1,0:T(8,128)(2,1)} %bitcast.36, f32[256,1024]{1,0:T(8,128)} %get-tuple-element.88.resid_ref, ...), custom_call_target="tpu_custom_call" | custom-call | tf_op jit(solution)/shard_map/finish/pallas_call | solution.py:1333
  302.7 0.7 dynamic-slice_convert_fusion
  303.4 0.6 reshape_squeeze.6
  304.0 0.6 reshape_squeeze.7
  304.5 0.0 copy-done.1
  304.6 0.5 slice_bitcast_fusion.1
  305.1 0.5 slice.33
  305.6 1.2 slice.34
  308.1 0.6 slice_bitcast_fusion
  308.7 0.0 copy-done
  308.7 0.8 copy.46
  (1 shorter events, 0.0 us)
Async XLA Ops:
  293.1 11.4 %copy-start.1 = (f32[16,128]{1,0:T(8,128)S(1)}, f32[16,128]{1,0:T(8,128)}, u32[]{:S(2)}) copy-start(f32[16,128]{1,0:T(8,128)} %get-tuple-element.84) | copy-start | bytes 24580
  293.1 15.5 %copy-start = (bf16[256,1024]{1,0:T(8,128)(2,1)S(1)}, bf16[256,1024]{1,0:T(8,128)(2,1)}, u32[]{:S(2)}) copy-start(bf16[256,1024]{1,0:T(8,128)(2,1)} %get-tuple-element.72) | copy-start | bytes 1572868
